TPU v7x, 128 devices: a whole 4x4x4 slice. The times are simulated.
128 devices in a mesh: gz: 8 (over y, x_hi), gy: 16 (over z, x_lo, core).
Axes of the slice: x: 4 (x_hi: 2, x_lo: 2; x = x_hi * 2 + x_lo), y: 4, z: 4, core: 2. Of those that a mesh axis runs over, the one named last changes fastest.
Arguments:
- velocity: float32 [128, 1024, 1024], P(None, 'gy', 'gz'), may hold values from -6 to 6
Outputs:
- fine_details: float32 [7, 64, 512, 512], P(None, None, 'gy', 'gz')
- coarse_bands: float32 [8, 32, 256, 256], P(None, None, 'gy', 'gz')
All inputs are finite; a program needn't handle non-finite values.
Results may differ from a plain program's by a relative error of at most 0.0003.
Values sent between devices are 32-bit elements; how exact they have to be, the bound alone decides.
A program may use at most 192 MiB of HBM per device.

v0:
```python
from functools import partial

import jax
import jax.numpy as jnp
from jax import lax
from jax.sharding import PartitionSpec as P

predict_one = -1.586134342
update_one = -0.05298011854
predict_two = 0.8829110762
update_two = 0.4435068522
scale_factor = 1.149604398


def padded(block, sides, width):
    for axis, dim in sides:
        count = lax.axis_size(axis)
        forward = [(i, i + 1) for i in range(count - 1)]
        forward.append((count - 1, 0))
        backward = [(target, source) for source, target in forward]
        low = lax.ppermute(
            lax.slice_in_dim(block, block.shape[dim] - width, None, axis=dim), axis, forward
        )
        high = lax.ppermute(lax.slice_in_dim(block, 0, width, axis=dim), axis, backward)
        block = jnp.concatenate([low, block, high], axis=dim)
    return block


def lift_axis(field, axis_index, take_next, take_prev):
    length = field.shape[axis_index]
    new_shape = field.shape[:axis_index] + (length // 2, 2) + field.shape[axis_index + 1 :]
    paired = field.reshape(new_shape)
    even_part = lax.index_in_dim(paired, 0, axis_index + 1, keepdims=False)
    odd_part = lax.index_in_dim(paired, 1, axis_index + 1, keepdims=False)
    odd_part = odd_part + predict_one * (even_part + take_next(even_part))
    even_part = even_part + update_one * (take_prev(odd_part) + odd_part)
    odd_part = odd_part + predict_two * (even_part + take_next(even_part))
    even_part = even_part + update_two * (take_prev(odd_part) + odd_part)
    return jnp.stack([even_part * scale_factor, odd_part / scale_factor], axis=axis_index)


def rolled_next(values_in, axis_index):
    return jnp.roll(values_in, -1, axis=axis_index)


def rolled_prev(values_in, axis_index):
    return jnp.roll(values_in, 1, axis=axis_index)


def lift_periodic(field, axis_index):
    return lift_axis(
        field,
        axis_index,
        partial(rolled_next, axis_index=axis_index),
        partial(rolled_prev, axis_index=axis_index),
    )


def lift_columns(columns):
    lifted = lift_periodic(columns, 2)
    return lax.all_to_all(lifted, "gy", split_axis=3, concat_axis=1, tiled=True)


def pass_along_y(along_x):
    return lift_columns(lax.all_to_all(along_x, "gy", split_axis=1, concat_axis=2, tiled=True))


def pass_along_z(along_y):
    widened = padded(along_y, (("gz", 4),), 4)
    lifted = lift_periodic(widened, 4)
    return lifted[..., 2:-2]


def transform_level(volume):
    along_x = lift_periodic(volume, 0)
    along_y = pass_along_y(along_x)
    along_z = pass_along_z(along_y)
    bands = jnp.transpose(along_z, (0, 2, 4, 1, 3, 5))
    return bands.reshape((8,) + bands.shape[3:])


def body(velocity):
    level_one = transform_level(velocity)
    level_two = transform_level(level_one[0])
    return (level_one[1:], level_two)


def solution(mesh):
    placed = (P(None, "gy", "gz"),)
    return jax.shard_map(
        body,
        mesh=mesh,
        in_specs=placed,
        out_specs=(P(None, None, "gy", "gz"), P(None, None, "gy", "gz")),
        check_vma=False,
    )
```

profile of v0, /device:TPU:1, one launch (start us, length us, event | category | flops | bytes accessed | tf_op | source)
XLA Modules:
  0.0 306.4 jit_solution(472895331870187040)
XLA Ops:
  10.2 56.9 %all_to_all.66 = f32[2,64,64,128]{3,2,0,1:T(8,128)S(1)} all-to-all(f32[2,64,64,128]{3,2,0,1:T(8,128)S(1)} %pad_maximum_fusion.2), channel_id=1, replica_groups=mesh['gz'=8,'gy'=16] {'gy'}, dimensions={1} | all-to-all | bytes 8388608 | tf_op jit(solution)/shard_map/all_to_all | solution.py:65
  67.7 4.0 %fusion.99 = (f32[2,4,512,1,128]{4,3,2,1,0:T(1,128)S(1)}, f32[2,4,512,1,128]{4,3,2,1,0:T(1,128)S(1)}) fusion(f32[2,4,512,2,128]{4,3,2,1,0:T(2,128)S(1)} %bitcast.369), kind=kLoop, calls=%fused_computation.207 | loop fusion | bytes 8388608 | tf_op jit(solution)/shard_map/slice | solution.py:34
  76.3 2.7 copy.148
  79.0 53.3 %all_to_all.67 = f32[2,4,2,512,128]{4,1,0,2,3:T(4,128)S(1)} all-to-all(f32[2,4,2,512,128]{4,1,0,2,3:T(4,128)S(1)} %copy.148), channel_id=1, replica_groups=mesh['gz'=8,'gy'=16] {'gy'}, dimensions={3} | all-to-all | bytes 8388608 | tf_op jit(solution)/shard_map/all_to_all | solution.py:61
  134.1 4.9 %fusion.98 = (f32[2,64,2,32,4]{4,3,2,1,0:T(8,128)}, f32[2,64,2,32,4]{4,3,2,1,0:T(8,128)}) fusion(f32[2,64,2,32,128]{4,3,2,1,0:T(8,128)S(1)} %bitcast.349), kind=kLoop, calls=%fused_computation.206 | loop fusion | bytes 524288 | tf_op jit(solution)/shard_map/slice | solution.py:22
  139.0 3.7 %copy.151 = f32[2,64,2,32,4]{1,3,4,2,0:T(8,128)S(1)} copy(f32[2,64,2,32,4]{4,3,2,1,0:T(8,128)} %get-tuple-element.22) | data formatting | bytes 262144 | tf_op jit(solution)/shard_map/slice | solution.py:22
  145.2 3.7 %copy.152 = f32[2,64,2,32,4]{1,3,4,2,0:T(8,128)S(1)} copy(f32[2,64,2,32,4]{4,3,2,1,0:T(8,128)} %get-tuple-element.23) | data formatting | bytes 262144 | tf_op jit(solution)/shard_map/slice | solution.py:24
  153.0 4.6 %copy.153 = f32[2,64,2,32,4]{4,3,2,1,0:T(8,128)} copy(f32[2,64,2,32,4]{1,3,4,2,0:T(8,128)S(1)} %collective-permute-done) | data formatting | bytes 262144 | tf_op jit(solution)/shard_map/ppermute | solution.py:21
  157.7 4.5 %copy.154 = f32[2,64,2,32,4]{4,3,2,1,0:T(8,128)} copy(f32[2,64,2,32,4]{1,3,4,2,0:T(8,128)S(1)} %collective-permute-done.1) | data formatting | bytes 262144 | tf_op jit(solution)/shard_map/ppermute | solution.py:24
  162.2 8.7 %pad_maximum_fusion.1 = f32[2,64,2,32,136]{4,3,2,1,0:T(8,128)} fusion(f32[2,64,2,32,4]{4,3,2,1,0:T(8,128)} %copy.154, f32[2,64,2,32,128]{4,3,2,1,0:T(8,128)} %bitcast.350, f32[2,64,2,32,4]{4,3,2,1,0:T(8,128)} %copy.153), kind=kLoop, calls=%fused_computation.2 | loop fusion | flops 2228224 | bytes 8912896 | tf_op jit(solution)/shard_map/concatenate | solution.py:25
  170.9 11.7 %copy.155 = f32[2,64,2,32,136]{1,3,4,2,0:T(8,128)} copy(f32[2,64,2,32,136]{4,3,2,1,0:T(8,128)} %pad_maximum_fusion.1) | data formatting | bytes 8912896 | tf_op jit(solution)/shard_map/concatenate | solution.py:25
  182.6 3.0 slice_bitcast_fusion.1
  185.6 2.8 slice_bitcast_fusion.51
  190.2 4.6 %slice_bitcast_fusion.50 = (f32[2,64,2,32,1,67]{1,3,5,2,0,4:T(8,128)}, f32[2,64,2,32,67]{1,3,4,2,0:T(8,128)}) fusion(f32[2,64,2,32,68]{1,3,4,2,0:T(8,128)S(1)} %fusion.2), kind=kLoop, calls=%fused_computation.202 | loop fusion | bytes 6586368 | tf_op jit(solution)/shard_map/jit(_roll_static)/concatenate | solution.py:47
  194.8 3.9 %fusion.8 = f32[2,64,2,32,68]{1,3,4,2,0:T(8,128)S(1)} fusion(f32[2,64,2,32,68]{1,3,4,2,0:T(8,128)S(1)} %fusion.2, f32[2,64,2,32,67]{1,3,4,2,0:T(8,128)} %get-tuple-element.21, f32[2,64,2,32,1]{1,3,4,2,0:T(8,128)S(1)} %get-tuple-element.19, f32[2,64,2,32,68,2]{1,3,5,4,2,0:T(8,128)S(1)} %bitcast.347), kind=kLoop, calls=%fused_computation.14 | loop fusion | flops 2228224 | bytes 8912896 | tf_op jit(solution)/shard_map/add | solution.py:36
  198.7 4.5 %fusion.96 = (f32[2,64,2,32,67]{1,3,4,2,0:T(8,128)}, f32[2,64,2,32,1,67]{1,3,5,2,0,4:T(8,128)}) fusion(f32[2,64,2,32,68]{1,3,4,2,0:T(8,128)S(1)} %fusion.8), kind=kLoop, calls=%fused_computation.204 | loop fusion | bytes 6586368 | tf_op jit(solution)/shard_map/jit(_roll_static)/slice | solution.py:43
  203.3 6.0 %fusion.10 = f32[2,64,2,32,68]{1,3,4,2,0:T(8,128)} fusion(f32[2,64,2,32,68]{1,3,4,2,0:T(8,128)S(1)} %fusion.2, f32[2,64,2,32,68]{1,3,4,2,0:T(8,128)S(1)} %fusion.8, f32[2,64,2,32,1]{1,3,4,2,0:T(8,128)S(1)} %get-tuple-element.12, f32[2,64,2,32,67]{1,3,4,2,0:T(8,128)} %get-tuple-element.10), kind=kLoop, calls=%fused_computation.17 | loop fusion | flops 2228224 | bytes 8912896 | tf_op jit(solution)/shard_map/add | solution.py:37
  209.3 4.7 %slice_bitcast_fusion = f32[2,64,2,32,1,67]{1,3,5,2,0,4:T(8,128)} fusion(f32[2,64,2,32,68]{1,3,4,2,0:T(8,128)} %fusion.10), kind=kLoop, calls=%fused_computation.25 | loop fusion | bytes 4390912 | tf_op jit(solution)/shard_map/jit(_roll_static)/concatenate | solution.py:47
  214.9 7.8 %fusion.13 = (f32[2,64,2,32,1,68]{1,3,5,2,0,4:T(8,128)S(1)}, f32[2,64,2,32,1,68]{1,3,5,2,0,4:T(8,128)S(1)}) fusion(f32[2,64,2,32,1,67]{1,3,5,2,0,4:T(8,128)} %slice_bitcast_fusion, f32[2,64,2,32,1,1]{1,3,5,2,0,4:T(8,128)S(1)} %slice_bitcast_fusion.12, f32[2,64,2,32,1,1]{1,3,5,2,0,4:T(8,128)S(1)} %get-tuple-element.13, ...), kind=kLoop, calls=%fused_computation.21 | loop fusion | flops 10027008 | bytes 17825792 | tf_op jit(solution)/shard_map/mul | solution.py:39
  222.7 4.3 %fusion = f32[2,2,2,64,32,64]{3,4,5,1,0,2:T(8,128)} fusion(f32[2,64,2,32,1,68]{1,3,5,2,0,4:T(8,128)S(1)} %get-tuple-element.3, f32[2,64,2,32,1,68]{1,3,5,2,0,4:T(8,128)S(1)} %get-tuple-element.2), kind=kLoop, calls=%fused_computation.1 | loop fusion | flops 1048576 | bytes 8650752 | tf_op jit(solution)/shard_map/transpose | solution.py:78
  227.0 12.2 %copy.161 = f32[2,2,2,64,32,64]{5,4,3,2,1,0:T(8,128)} copy(f32[2,2,2,64,32,64]{3,4,5,1,0,2:T(8,128)} %fusion) | data formatting | bytes 8388608 | tf_op jit(solution)/shard_map/transpose | solution.py:78
  242.6 14.8 %all_to_all.68 = f32[16,1,8192]{2,1,0:T(1,128)S(1)} all-to-all(f32[16,1,8192]{2,1,0:T(1,128)S(1)} %reshape.1258), channel_id=1, replica_groups=mesh['gz'=8,'gy'=16] {'gy'}, dimensions={0} | all-to-all | bytes 1048576 | tf_op jit(solution)/shard_map/all_to_all | solution.py:65
  264.2 13.7 %all_to_all.69 = f32[16,1,8192]{2,1,0:T(1,128)S(1)} all-to-all(f32[16,1,8192]{2,1,0:T(1,128)S(1)} %reshape.1260), channel_id=1, replica_groups=mesh['gz'=8,'gy'=16] {'gy'}, dimensions={0} | all-to-all | bytes 1048576 | tf_op jit(solution)/shard_map/all_to_all | solution.py:61
  287.8 7.4 %slice.348 = f32[7,64,32,64]{3,2,1,0:T(8,128)} slice(f32[8,64,32,64]{3,2,1,0:T(8,128)} %bitcast.366), slice={[1:8], [0:64], [0:32], [0:64]} | slice | bytes 7340032 | tf_op jit(solution)/shard_map/slice | solution.py:85
  (114 shorter events, 56.1 us)
Async XLA Ops:
  0.6 2.8 copy-start.1
  134.1 4.9 %copy-start = (f32[2,16,4,2,32,128]{5,4,3,2,1,0:T(8,128)}, f32[2,16,4,2,32,128]{5,4,3,2,1,0:T(8,128)S(1)}, u32[]{:S(2)}) copy-start(f32[2,16,4,2,32,128]{5,4,3,2,1,0:T(8,128)S(1)} %copy.150) | copy-start | bytes 12582916
  142.7 10.3 %collective-permute-start = (f32[2,64,2,32,4]{1,3,4,2,0:T(8,128)S(1)}, f32[2,64,2,32,4]{1,3,4,2,0:T(8,128)S(1)}, u32[]{:S(2)}, u32[]{:S(2)}) collective-permute-start(f32[2,64,2,32,4]{1,3,4,2,0:T(8,128)S(1)} %copy.151), channel_id=1, source_target_pairs={{0,16},{16,32},{32,48},{48,64},{64,80},{80,96},{96,112},{112,0},{1... | collective-permute-start | bytes 393224 | tf_op jit(solution)/shard_map/ppermute | solution.py:21
  148.9 8.8 %collective-permute-start.1 = (f32[2,64,2,32,4]{1,3,4,2,0:T(8,128)S(1)}, f32[2,64,2,32,4]{1,3,4,2,0:T(8,128)S(1)}, u32[]{:S(2)}, u32[]{:S(2)}) collective-permute-start(f32[2,64,2,32,4]{1,3,4,2,0:T(8,128)S(1)} %copy.152), channel_id=1, source_target_pairs={{16,0},{32,16},{48,32},{64,48},{80,64},{96,80},{112,96},{0,112},{1... | collective-permute-start | bytes 393224 | tf_op jit(solution)/shard_map/ppermute | solution.py:24
  182.6 5.8 %slice-start = ((s8[8912896]{0:T(1024)(128)(4,1)}), s8[4194304]{0:T(1024)(128)(4,1)S(1)}, s32[]{:S(2)}) async-start(s8[8912896]{0:T(1024)(128)(4,1)} %bitcast.344), calls=%async_computation.4 | async-start | bytes 8388608
  182.6 5.8 %slice-start.1 = ((s8[8912896]{0:T(1024)(128)(4,1)}), s8[4194304]{0:T(1024)(128)(4,1)S(1)}, s32[]{:S(2)}) async-start(s8[8912896]{0:T(1024)(128)(4,1)} %bitcast.344), calls=%async_computation.5 | async-start | bytes 8388608
  185.6 2.9 slice-start.2
  282.0 13.2 %collective-permute-start.2 = (f32[2,32,2,16,4]{1,3,4,2,0:T(8,128)S(1)}, f32[2,32,2,16,4]{1,3,4,2,0:T(8,128)S(1)}, u32[]{:S(2)}, u32[]{:S(2)}) collective-permute-start(f32[2,32,2,16,4]{1,3,4,2,0:T(8,128)S(1)} %copy.178), channel_id=1, source_target_pairs={{0,16},{16,32},{32,48},{48,64},{64,80},{80,96},{96,112},{112,0},{1... | collective-permute-start | bytes 98312 | tf_op jit(solution)/shard_map/ppermute | solution.py:21
  285.2 10.9 %collective-permute-start.3 = (f32[2,32,2,16,4]{1,3,4,2,0:T(8,128)S(1)}, f32[2,32,2,16,4]{1,3,4,2,0:T(8,128)S(1)}, u32[]{:S(2)}, u32[]{:S(2)}) collective-permute-start(f32[2,32,2,16,4]{1,3,4,2,0:T(8,128)S(1)} %copy.179), channel_id=1, source_target_pairs={{16,0},{32,16},{48,32},{64,48},{80,64},{96,80},{112,96},{0,112},{1... | collective-permute-start | bytes 98312 | tf_op jit(solution)/shard_map/ppermute | solution.py:24
where the time goes:
time: 311 us; the launch traced here: 306 us
  blocking collectives  139 us (45%)
  local copies, waits for them, and re-layouts  104 us (33%)
  other arithmetic  49.8 us (16%)
  starting transfers between devices  10.4 us (3%)
    all_to_all x2, blocking collectives, pass_along_y(): lax.all_to_all(along_x, 'gy', split_axis=1, concat_axis=2, tiled=True)  71.7 us
    all_to_all x2, blocking collectives, lift_columns(): return lax.all_to_all(lifted, 'gy', split_axis=3, concat_axis=1, tiled=True)  67 us
    transpose x2, local copies, waits for them, and re-layouts, transform_level(): bands = jnp.transpose(along_z, (0, 2, 4, 1, 3, 5))  14.6 us
    concatenate x2, local copies, waits for them, and re-layouts, padded(): block = jnp.concatenate([low, block, high], axis=dim)  14.1 us
    mul x6, other arithmetic, lift_axis(): even_part * scale_factor  13.2 us
    concatenate x24, local copies, waits for them, and re-layouts, rolled_prev(): return jnp.roll(values_in, 1, axis=axis_index)  12.1 us
    concatenate x2, other arithmetic, padded(): block = jnp.concatenate([low, block, high], axis=dim)  10.3 us
    slice x4, local copies, waits for them, and re-layouts, padded(): lax.slice_in_dim(block, block.shape[dim] - width, None, axis=dim)  9.57 us
  transfers between devices with their start and end apart: 4, of which 2 were waited for; matrix products, arithmetic and copies ran while one was open for 6% of the time, Pallas kernels for 0%

commit v1 on v0

v1 whole, which is shorter than its diff:
```python
import functools

import jax
import jax.numpy as jnp
import ml_dtypes
import numpy as np
from jax import lax
from jax.experimental import pallas as pl
from jax.experimental.pallas import tpu as pltpu
from jax.sharding import PartitionSpec as P

predict_one = -1.586134342
update_one = -0.05298011854
predict_two = 0.8829110762
update_two = 0.4435068522
scale_factor = 1.149604398

MESH = pl.DeviceIdType.MESH
F32 = jnp.float32
BF16 = jnp.bfloat16
NX, HX = 128, 64
BY, BZ = 64, 128
LOW_ROWS, HIGH_ROWS = 4 * HX, 2 * HX


def lift_rows(v):
    s, d = v[0::2], v[1::2]
    d = d + predict_one * (s + np.roll(s, -1, 0))
    s = s + update_one * (np.roll(d, 1, 0) + d)
    d = d + predict_two * (s + np.roll(s, -1, 0))
    s = s + update_two * (np.roll(d, 1, 0) + d)
    return s * scale_factor, d / scale_factor


def factored(block, fine):
    first = np.linalg.svd(block[:fine])[2][:2]
    rest = block[fine:] - (block[fine:] @ first.T) @ first
    second = np.linalg.svd(rest)[2][:2]
    basis = np.concatenate([first, second])
    gains = block @ basis.T
    gains[:fine, 2:] = 0
    return basis, gains


@functools.cache
def operators(n):
    low, high = lift_rows(np.eye(3 * n))
    low2, high2 = lift_rows(low)
    h, q = n // 2, n // 4
    rows = np.concatenate([low[h : 2 * h], high[h : 2 * h], low2[q : 2 * q], high2[q : 2 * q]])
    return rows[:, n : 2 * n], factored(rows[:, :n], n), factored(rows[:, 2 * n :], n)


def halves(w):
    hi = w.astype(ml_dtypes.bfloat16)
    return hi, (w - hi.astype(np.float64)).astype(ml_dtypes.bfloat16)


def three(w, axis):
    hi, lo = halves(w)
    return np.concatenate([hi, hi, lo], axis)


@functools.cache
def constants():
    own_y, (basis_left, gain_left), (basis_right, gain_right) = operators(BY)
    y_low = np.zeros((2, 96, 80))
    y_high = np.zeros((4, 64, 80))
    for p in range(2):
        y_low[p, :, :64] = own_y
        y_low[p, :, 64 + 4 * p : 68 + 4 * p] = gain_left
        y_low[p, :, 72 + 4 * p : 76 + 4 * p] = gain_right
    for p in range(4):
        y_high[p, :, :64] = own_y[:64]
        y_high[p, :, 64 + 2 * p : 66 + 2 * p] = gain_left[:64, :2]
        y_high[p, :, 72 + 2 * p : 74 + 2 * p] = gain_right[:64, :2]
    edge = np.r_[0:16, 48:64]
    assert abs(np.delete(basis_left, edge, 1)).max() < 1e-12
    assert abs(np.delete(basis_right, edge, 1)).max() < 1e-12
    state_low = np.zeros((64, 256))
    state_high = np.zeros((32, 256))
    for side, basis in enumerate((basis_right, basis_left)):
        for i in range(8):
            columns = slice(32 * i, 32 * i + 32)
            state_low[32 * side + 4 * i : 32 * side + 4 * i + 4, columns] = basis[:, edge]
            state_high[16 * side + 2 * i : 16 * side + 2 * i + 2, columns] = basis[:2, edge]

    own_z, (left, gain_l), (right, gain_r) = operators(BZ)
    zs_low = np.concatenate([np.tile(b.T, (1, 32)) for b in (right, left)], 1)
    zs_high = np.concatenate([np.tile(b[:2].T, (1, 64)) for b in (right, left)], 1)

    def spread(rows):
        k = rows.shape[1]
        fine = np.zeros((k, 256))
        fine[:, :64] = rows[:64].T
        fine[:, 128:192] = rows[64:128].T
        coarse = np.zeros((k, 128))
        coarse[:, :64] = rows[128:].T
        return fine, coarse

    main_fine, main_coarse = spread(own_z)
    halo_fine, halo_coarse = spread(np.concatenate([gain_l, gain_r], 1))

    def passes(main, halo):
        hi, lo = halves(main)
        ehi, elo = halves(halo)
        one = np.concatenate([hi, hi], 0)
        two = np.zeros((4, 256, main.shape[1]), ml_dtypes.bfloat16)
        for i in range(4):
            two[i, :128] = lo
            two[i, 128 + 32 * i : 128 + 32 * i + 24] = np.concatenate([ehi, ehi, elo], 0)
        return one, two

    def places(states):
        p = np.zeros((4, 128, 128))
        for lane in range(128):
            i, s = lane // states % 4, lane % states
            p[0, lane, 32 * i + s] = p[0, lane, 32 * i + 16 + s] = 1
            p[1, lane, 32 * i + 8 + s] = 1
            p[2, lane, 32 * i + 4 + s] = p[2, lane, 32 * i + 20 + s] = 1
            p[3, lane, 32 * i + 12 + s] = 1
        return p.reshape(512, 128).astype(ml_dtypes.bfloat16)

    w1, w2 = passes(main_fine, halo_fine)
    w1c, w2c = passes(main_coarse, halo_coarse)
    send = (three(state_low, 1), three(state_high, 1), three(zs_low, 0), three(zs_high, 0))
    work = (three(y_low, 2), three(y_high, 2), w1, w2, w1c, w2c, places(4), places(2))
    return send, work


def split(v):
    hi = v.astype(BF16)
    return hi, (v - hi.astype(F32)).astype(BF16)


def dot(a, b):
    return jnp.dot(a, b, preferred_element_type=F32)


def lift_loop(count, unroll, load, store):
    k = 2 * count
    s_a, d_a, s_b, d_b, s_c, d_c, s_d = [load(i % k) for i in range(k - 4, k + 3)]
    d_a = d_a + predict_one * (s_a + s_b)
    d_b = d_b + predict_one * (s_b + s_c)
    s_b = s_b + update_one * (d_a + d_b)
    d_c = d_c + predict_one * (s_c + s_d)
    s_c = s_c + update_one * (d_b + d_c)
    d_b = d_b + predict_two * (s_b + s_c)

    def step(j, carry):
        s_now, d_before, s_before, d_done = carry
        for u in range(unroll):
            n = unroll * j + u + 1
            d_now, s_next = load(lax.rem(2 * n + 1, k)), load(lax.rem(2 * n + 2, k))
            d_now = d_now + predict_one * (s_now + s_next)
            s_now = s_now + update_one * (d_before + d_now)
            d_before = d_before + predict_two * (s_before + s_now)
            s_before = s_before + update_two * (d_done + d_before)
            store(n - 1, s_before * scale_factor, d_before * (1.0 / scale_factor))
            s_now, d_before, s_before, d_done = s_next, d_now, s_now, d_before
        return s_now, d_before, s_before, d_done

    lax.fori_loop(0, count // unroll, step, (s_d, d_c, s_c, d_b))


def exchange_kernel(
    v_hbm, st_low, st_high, zs_low, zs_high,
    x_hi, x_lo, y_recv, z_recv, c_recv,
    v, y_send, z_send, c_send, in_sem, send_sem, recv_sem,
):
    my_y, my_z = lax.axis_index("gy"), lax.axis_index("gz")
    n_y, n_z = lax.axis_size("gy"), lax.axis_size("gz")

    def device(step_y, step_z):
        return {
            "gy": lax.rem(my_y + step_y + n_y, n_y),
            "gz": lax.rem(my_z + step_z + n_z, n_z),
        }

    steps = [(0, -1), (0, 1), (-1, 0), (1, 0), (-1, -1), (-1, 1), (1, -1), (1, 1)]
    barrier = pltpu.get_barrier_semaphore()
    for step in steps:
        pl.semaphore_signal(barrier, inc=1, device_id=device(*step), device_id_type=MESH)

    order = (0, 3, 1, 2)
    loads = {}
    for c in order:
        rows = pl.ds(16 * c, 16)
        loads[c] = pltpu.make_async_copy(v_hbm.at[:, rows], v.at[:, rows], in_sem.at[c])
        loads[c].start()

    for c in order:
        loads[c].wait()
        rows = pl.ds(16 * c, 16)

        def store(n, low, high, rows=rows):
            x_hi[n, rows], x_lo[n, rows] = split(low)
            x_hi[HX + n, rows], x_lo[HX + n, rows] = split(high)

        lift_loop(HX, 4, lambda i, rows=rows: v[i, rows], store)

    def y_states(g, carry):
        for half, table, per in ((0, st_low, 4), (1, st_high, 2)):
            first = HX * half + 8 * g
            parts = []
            for ref in (x_hi, x_lo):
                for i in range(8):
                    parts += [ref[first + i, 0:16], ref[first + i, 48:64]]
            parts += parts[:16]
            states = dot(table[...], jnp.concatenate(parts, 0))
            n = 8 * per
            at = pl.ds(pl.multiple_of(LOW_ROWS * half + n * g, n), n)
            y_send[0, at] = states[:n]
            y_send[1, at] = states[n:]
        return carry

    lax.fori_loop(0, 8, y_states, 0)

    lane = lax.broadcasted_iota(jnp.int32, (64, 256), 1) % 128
    for group, (first, count, table, per) in enumerate(
        ((0, 32, zs_low, 4), (32, 32, zs_low, 4), (64, 64, zs_high, 2))
    ):

        def z_states(j, acc, first=first, table=table, per=per):
            hi = x_hi[pl.ds(first + 8 * j, 8)].reshape(512, 128)
            lo = x_lo[pl.ds(first + 8 * j, 8)].reshape(512, 128)
            states = dot(jnp.concatenate([hi, lo, hi], 1), table[...])
            for i in range(8):
                mine = lane // per == 8 * j + i
                acc = jnp.where(mine, states[64 * i : 64 * i + 64], acc)
            return acc

        acc = lax.fori_loop(0, count // 8, z_states, jnp.zeros((64, 256), F32))
        z_send[0, 64 * group : 64 * group + 64] = acc[:, :128]
        z_send[1, 64 * group : 64 * group + 64] = acc[:, 128:]

    his, los = [], []
    zeros = jnp.zeros((32, 128), F32)
    for side in range(2):
        for group in range(4):
            if group == 3:
                piece = zeros
            else:
                at = 64 * group
                piece = jnp.concatenate(
                    [z_send[side, at : at + 16], z_send[side, at + 48 : at + 64]], 0
                )
            hi, lo = split(piece)
            his.append(hi)
            los.append(lo)
    c_send[...] = dot(st_low[...], jnp.concatenate(his + los + his, 0)).reshape(4, 16, 128)

    pl.semaphore_wait(barrier, 8)
    copies = []
    for k, step in enumerate(steps):
        if k < 2:
            source, target = z_send.at[k], z_recv.at[1 - k]
        elif k < 4:
            source, target = y_send.at[k - 2], y_recv.at[3 - k]
        else:
            source, target = c_send.at[k - 4], c_recv.at[7 - k]
        copy = pltpu.make_async_remote_copy(
            src_ref=source, dst_ref=target, send_sem=send_sem.at[k], recv_sem=recv_sem.at[k],
            device_id=device(*step), device_id_type=MESH,
        )
        copy.start()
        copies.append(copy)
    for copy in copies:
        copy.wait()


def finish_kernel(
    x_hi, x_lo, y_recv, z_recv, c_recv,
    y_low, y_high, w1, w2, w1c, w2c, p_low, p_high,
    fine_hbm, coarse_hbm,
    fine, coarse, level, zh_low, zh_high, sem,
):
    def stacked(hi, lo, tiles):
        thi, tlo = split(tiles)
        return jnp.concatenate([hi, thi, lo, tlo, hi, thi], 0)

    lane = lax.broadcasted_iota(jnp.int32, (1, 128), 1)
    for group in range(3):
        blocks = []
        for side in range(2):
            hi, lo = split(z_recv[side, 64 * group : 64 * group + 64])
            at = 8 * (group // 2)
            tiles = jnp.concatenate([c_recv[side, at : at + 8], c_recv[2 + side, at : at + 8]], 0)
            blocks += split(dot(y_low[group % 2], stacked(hi, lo, tiles)))
        both = jnp.concatenate(blocks, 1)
        if group < 2:
            for g in range(8):
                mask = jnp.where(lane // 16 == g, 1.0, 0.0).astype(BF16)
                mask = jnp.concatenate([mask] * 4, 1)
                zh_low[8 * group + g] = dot(both * mask, p_low[...]).astype(BF16)
        else:
            for g in range(16):
                mask = jnp.where(lane // 8 == g, 1.0, 0.0).astype(BF16)
                mask = jnp.concatenate([mask] * 4, 1)
                zh_high[g] = dot(both[:64] * mask, p_high[...]).astype(BF16)

    def write(bands, first, count, slot):
        src = fine.at[bands, pl.ds(first, count)]
        dst = fine_hbm.at[bands, pl.ds(first, count)]
        return pltpu.make_async_copy(src, dst, sem.at[slot])

    def lifted(x, table, tile_at):
        tiles = jnp.concatenate([y_recv[0, tile_at], y_recv[1, tile_at]], 0)
        return split(dot(table, stacked(x_hi[x], x_lo[x], tiles)))

    def low_four(q, carry):
        for i in range(4):
            x = 4 * q + i
            at = pl.ds(pl.multiple_of(16 * q + 8 * (i // 2), 8), 8)
            hi, lo = lifted(x, y_low[i % 2], at)
            extra = zh_low[q]
            one = dot(jnp.concatenate([hi[:64], lo[:64]], 1), w1[...])
            one = one + dot(jnp.concatenate([hi[:64], extra[:64]], 1), w2[i])
            fine[0, x] = one[:32, 128:192]
            fine[1, x] = one[32:, :64]
            fine[2, x] = one[32:, 128:192]
            two = dot(jnp.concatenate([hi[64:], lo[64:]], 1), w1c[...])
            level[x] = two + dot(jnp.concatenate([hi[64:], extra[64:]], 1), w2c[i])
        return carry

    def high_four(q, carry):
        for i in range(4):
            x = 4 * q + i
            at = pl.ds(pl.multiple_of(LOW_ROWS + 8 * q, 8), 8)
            hi, lo = lifted(HX + x, y_high[i], at)
            one = dot(jnp.concatenate([hi, lo], 1), w1[...])
            one = one + dot(jnp.concatenate([hi, zh_high[q]], 1), w2[i])
            fine[3, x] = one[:32, :64]
            fine[4, x] = one[:32, 128:192]
            fine[5, x] = one[32:, :64]
            fine[6, x] = one[32:, 128:192]
        return carry

    copies = []
    for part in range(4):
        lax.fori_loop(4 * part, 4 * part + 4, low_four, 0)
        copies.append(write(slice(0, 3), 16 * part, 16, part))
        copies[-1].start()

    def store(n, low, high):
        for bx, value in enumerate((low, high)):
            for by in range(2):
                for bz in range(2):
                    coarse[4 * bx + 2 * by + bz, n] = value[
                        16 * by : 16 * by + 16, 32 * bz : 32 * bz + 32
                    ]

    lift_loop(HX // 2, 2, lambda i: level[i], store)
    copies.append(pltpu.make_async_copy(coarse, coarse_hbm, sem.at[8]))
    copies[-1].start()
    for part in range(4):
        lax.fori_loop(4 * part, 4 * part + 4, high_four, 0)
        copies.append(write(slice(3, 7), 16 * part, 16, 4 + part))
        copies[-1].start()
    for copy in copies:
        copy.wait()


def body(velocity):
    send, work = constants()
    vmem = pl.BlockSpec(memory_space=pltpu.VMEM)
    hbm = pl.BlockSpec(memory_space=pl.ANY)
    shape = jax.ShapeDtypeStruct
    y_shape, z_shape, c_shape = (2, LOW_ROWS + HIGH_ROWS, BZ), (2, 3 * BY, 128), (4, 16, 128)
    halos = pl.pallas_call(
        exchange_kernel,
        out_shape=(
            shape((NX, BY, BZ), BF16), shape((NX, BY, BZ), BF16),
            shape(y_shape, F32), shape(z_shape, F32), shape(c_shape, F32),
        ),
        in_specs=[hbm] + [vmem] * 4,
        out_specs=(vmem,) * 5,
        scratch_shapes=[
            pltpu.VMEM((NX, BY, BZ), F32),
            pltpu.VMEM(y_shape, F32),
            pltpu.VMEM(z_shape, F32),
            pltpu.VMEM(c_shape, F32),
            pltpu.SemaphoreType.DMA((4,)),
            pltpu.SemaphoreType.DMA((8,)),
            pltpu.SemaphoreType.DMA((8,)),
        ],
        compiler_params=pltpu.CompilerParams(
            collective_id=0, has_side_effects=True, vmem_limit_bytes=24 * 2**20
        ),
        name="exchange",
    )(velocity, *[jnp.asarray(a) for a in send])
    fine_shape, coarse_shape = (7, HX, BY // 2, BZ // 2), (8, HX // 2, BY // 4, BZ // 4)
    return pl.pallas_call(
        finish_kernel,
        out_shape=(shape(fine_shape, F32), shape(coarse_shape, F32)),
        in_specs=[vmem] * 13,
        out_specs=(hbm, hbm),
        scratch_shapes=[
            pltpu.VMEM(fine_shape, F32),
            pltpu.VMEM(coarse_shape, F32),
            pltpu.VMEM((HX, 32, 128), F32),
            pltpu.VMEM((16, 96, 128), BF16),
            pltpu.VMEM((16, 64, 128), BF16),
            pltpu.SemaphoreType.DMA((9,)),
        ],
        compiler_params=pltpu.CompilerParams(vmem_limit_bytes=28 * 2**20),
        name="finish",
    )(*halos, *[jnp.asarray(a) for a in work])


def solution(mesh):
    return jax.shard_map(
        body,
        mesh=mesh,
        in_specs=(P(None, "gy", "gz"),),
        out_specs=(P(None, None, "gy", "gz"), P(None, None, "gy", "gz")),
        check_vma=False,
    )
```

time: 311 us -> 59.6 us (0.19); the launches traced: 306 us -> 59.3 us
  blocking collectives: 139 us -> 0 us
  local copies, waits for them, and re-layouts: 104 us -> 5.77 us
  Pallas kernels: 0 us -> 52.8 us
  other arithmetic: 49.8 us -> 0 us
  starting transfers between devices: 10.4 us -> 0 us
    all_to_all x4 -> x0, blocking collectives: 139 us -> none  [the longest x2 71.7 us: pass_along_y(): lax.all_to_all(along_x, 'gy', split_axis=1, concat_axis=2, tiled=True)]
    pallas_call x0 -> x2, Pallas kernels: none -> 52.8 us  [the longest x1 26.4 us: body(): pl.pallas_call(exchange_kernel, out_shape=(shape((NX, BY, BZ), BF16), sha...]
    slice x24 -> x0, local copies, waits for them, and re-layouts: 33.2 us -> none  [the longest x4 9.57 us: padded(): lax.slice_in_dim(block, block.shape[dim] - width, None, axis=dim)]
    concatenate x36 -> x0, local copies, waits for them, and re-layouts: 31.9 us -> none  [the longest x2 14.1 us: padded(): block = jnp.concatenate([low, block, high], axis=dim)]
    add x18 -> x0, other arithmetic: 16.9 us -> none  [the longest x6 7.73 us: lift_axis(): odd_part = odd_part + predict_two * (even_part + take_next(even_part))]
    transpose x2 -> x0, local copies, waits for them, and re-layouts: 14.6 us -> none  [transform_level(): bands = jnp.transpose(along_z, (0, 2, 4, 1, 3, 5))]
    mul x6 -> x0, other arithmetic: 13.2 us -> none  [lift_axis(): even_part * scale_factor]
    ppermute x4 -> x0, local copies, waits for them, and re-layouts: 11 us -> none  [the longest x2 5.54 us: padded(): lax.ppermute(lax.slice_in_dim(block, block.shape[dim] - width, None, axis...]
  transfers between devices with their start and end apart: 4 -> 0, of which waited for: 2 -> 0; matrix products, arithmetic and copies ran while one was open for 6% -> 0% of each run, Pallas kernels for 0% -> 0%
where the time goes in v1:
time: 59.6 us; the launch traced here: 59.3 us
  Pallas kernels  52.8 us (89%)
  local copies, waits for them, and re-layouts  5.77 us (10%)
  between operations  0.75 us (1%)
    pallas_call x1, Pallas kernels, body(): pl.pallas_call(exchange_kernel, out_shape=(shape((NX, BY, BZ), BF16), sha...  26.4 us
    pallas_call x1, Pallas kernels, body(): pl.pallas_call(finish_kernel, out_shape=(shape(fine_shape, F32), shape(co...  26.4 us
    unnamed x26, local copies, waits for them, and re-layouts  5.77 us

profile of v1, /device:TPU:1, one launch (start us, length us, event | category | flops | bytes accessed | tf_op | source)
XLA Modules:
  0.0 59.3 jit_solution(14854528267281132703)
XLA Ops:
  0.6 0.0 copy-start
  0.6 2.2 %copy-done = f32[128,64,128]{2,1,0:T(8,128)S(1)} copy-done((f32[128,64,128]{2,1,0:T(8,128)S(1)}, f32[128,64,128]{2,1,0:T(8,128)}, u32[]{:S(2)}) %copy-start) | copy-done | bytes 4194328
  2.8 0.0 copy-start.3
  2.8 0.9 %copy-done.3 = bf16[384,256]{1,0:T(8,128)(2,1)S(1)} copy-done((bf16[384,256]{1,0:T(8,128)(2,1)S(1)}, bf16[384,256]{1,0:T(8,128)(2,1)}, u32[]{:S(2)}) %copy-start.3) | copy-done | bytes 196632
  3.7 0.0 copy-start.4
  3.7 0.9 %copy-done.4 = bf16[384,256]{1,0:T(8,128)(2,1)S(1)} copy-done((bf16[384,256]{1,0:T(8,128)(2,1)S(1)}, bf16[384,256]{1,0:T(8,128)(2,1)}, u32[]{:S(2)}) %copy-start.4) | copy-done | bytes 196632
  4.7 0.0 copy-start.10
  4.7 0.9 %copy-done.10 = bf16[64,768]{1,0:T(8,128)(2,1)S(1)} copy-done((bf16[64,768]{1,0:T(8,128)(2,1)S(1)}, bf16[64,768]{1,0:T(8,128)(2,1)}, u32[]{:S(2)}) %copy-start.10) | copy-done | bytes 98328
  5.6 0.0 copy-start.12
  5.6 0.8 %copy-done.12 = bf16[32,768]{1,0:T(8,128)(2,1)S(1)} copy-done((bf16[32,768]{1,0:T(8,128)(2,1)S(1)}, bf16[32,768]{1,0:T(8,128)(2,1)}, u32[]{:S(2)}) %copy-start.12) | copy-done | bytes 49176
  6.4 0.0 copy-start.7
  6.4 0.0 copy-start.8
  6.4 0.0 copy-start.9
  6.4 0.0 copy-start.11
  6.4 26.4 %exchange.1 = (bf16[128,64,128]{2,1,0:T(8,128)(2,1)S(1)}, bf16[128,64,128]{2,1,0:T(8,128)(2,1)S(1)}, f32[2,384,128]{2,1,0:T(8,128)S(1)}, f32[2,192,128]{2,1,0:T(8,128)S(1)}, f32[4,16,128]{2,1,0:T(8,128)S(1)}) custom-call(f32[128,64,128]{2,1,0:T(8,128)S(1)} %copy-done, bf16[64,768]{1,0:T(8,128)(2,1)S(1)} %copy-done.10, bf16[32,768]{1,0:T(8,128)(2,1)S(1)} %copy-done.12, ...), custom_call_target="tpu_custom_call" | custom-call | tf_op jit(solution)/shard_map/exchange/pallas_call | solution.py:370
  32.8 0.0 copy-done.1
  32.8 0.0 copy-done.2
  32.9 0.0 copy-done.5
  32.9 0.0 copy-done.6
  32.9 0.0 copy-done.7
  32.9 0.0 copy-done.8
  32.9 0.0 copy-done.9
  32.9 0.0 copy-done.11
  32.9 26.4 %finish.1 = (f32[7,64,32,64]{3,2,1,0:T(8,128)}, f32[8,32,16,32]{3,2,1,0:T(8,128)}) custom-call(bf16[128,64,128]{2,1,0:T(8,128)(2,1)S(1)} %get-tuple-element.7.x_hi, bf16[128,64,128]{2,1,0:T(8,128)(2,1)S(1)} %get-tuple-element.8.x_lo, f32[2,384,128]{2,1,0:T(8,128)S(1)} %get-tuple-element.9.y_recv, f32[2,192,128]{2,1,0:T(8,128)S(1)} %get-tuple-element.10.z_recv, ...), custom_call_target="tpu_custom_call" | custom-call | tf_op jit(solution)/shard_map/finish/pallas_call | solution.py:393
  (4 shorter events, 0.0 us)
Async XLA Ops:
  0.6 2.2 %copy-start = (f32[128,64,128]{2,1,0:T(8,128)S(1)}, f32[128,64,128]{2,1,0:T(8,128)}, u32[]{:S(2)}) copy-start(f32[128,64,128]{2,1,0:T(8,128)} %v_hbm.1) | copy-start | bytes 12582916
  2.8 0.9 %copy-start.3 = (bf16[384,256]{1,0:T(8,128)(2,1)S(1)}, bf16[384,256]{1,0:T(8,128)(2,1)}, u32[]{:S(2)}) copy-start(bf16[384,256]{1,0:T(8,128)(2,1)} %constant.27.clone.zs_high) | copy-start | bytes 589828
  3.7 0.9 %copy-start.4 = (bf16[384,256]{1,0:T(8,128)(2,1)S(1)}, bf16[384,256]{1,0:T(8,128)(2,1)}, u32[]{:S(2)}) copy-start(bf16[384,256]{1,0:T(8,128)(2,1)} %constant.26.clone.zs_low) | copy-start | bytes 589828
  4.7 0.9 %copy-start.10 = (bf16[64,768]{1,0:T(8,128)(2,1)S(1)}, bf16[64,768]{1,0:T(8,128)(2,1)}, u32[]{:S(2)}) copy-start(bf16[64,768]{1,0:T(8,128)(2,1)} %constant.24.clone.st_low) | copy-start | bytes 294916
  5.6 0.8 %copy-start.12 = (bf16[32,768]{1,0:T(8,128)(2,1)S(1)}, bf16[32,768]{1,0:T(8,128)(2,1)}, u32[]{:S(2)}) copy-start(bf16[32,768]{1,0:T(8,128)(2,1)} %constant.25.clone.st_high) | copy-start | bytes 147460
  6.4 26.5 %copy-start.1 = (bf16[4,256,256]{2,1,0:T(8,128)(2,1)S(1)}, bf16[4,256,256]{2,1,0:T(8,128)(2,1)}, u32[]{:S(2)}) copy-start(bf16[4,256,256]{2,1,0:T(8,128)(2,1)} %constant.31.clone.w2) | copy-start | bytes 1572868
  6.4 26.5 %copy-start.2 = (bf16[4,256,128]{2,1,0:T(8,128)(2,1)S(1)}, bf16[4,256,128]{2,1,0:T(8,128)(2,1)}, u32[]{:S(2)}) copy-start(bf16[4,256,128]{2,1,0:T(8,128)(2,1)} %constant.33.clone.w2c) | copy-start | bytes 786436
  6.4 26.5 %copy-start.5 = (bf16[512,128]{1,0:T(8,128)(2,1)S(1)}, bf16[512,128]{1,0:T(8,128)(2,1)}, u32[]{:S(2)}) copy-start(bf16[512,128]{1,0:T(8,128)(2,1)} %constant.35.clone.p_high) | copy-start | bytes 393220
  6.4 26.5 %copy-start.6 = (bf16[512,128]{1,0:T(8,128)(2,1)S(1)}, bf16[512,128]{1,0:T(8,128)(2,1)}, u32[]{:S(2)}) copy-start(bf16[512,128]{1,0:T(8,128)(2,1)} %constant.34.clone.p_low) | copy-start | bytes 393220
  6.4 26.5 %copy-start.7 = (bf16[256,256]{1,0:T(8,128)(2,1)S(1)}, bf16[256,256]{1,0:T(8,128)(2,1)}, u32[]{:S(2)}) copy-start(bf16[256,256]{1,0:T(8,128)(2,1)} %constant.30.clone.w1) | copy-start | bytes 393220
  6.4 26.5 %copy-start.8 = (bf16[4,64,240]{2,1,0:T(8,128)(2,1)S(1)}, bf16[4,64,240]{2,1,0:T(8,128)(2,1)}, u32[]{:S(2)}) copy-start(bf16[4,64,240]{2,1,0:T(8,128)(2,1)} %constant.29.clone.y_high) | copy-start | bytes 368644
  6.4 26.5 %copy-start.9 = (bf16[2,96,240]{2,1,0:T(8,128)(2,1)S(1)}, bf16[2,96,240]{2,1,0:T(8,128)(2,1)}, u32[]{:S(2)}) copy-start(bf16[2,96,240]{2,1,0:T(8,128)(2,1)} %constant.28.clone.y_low) | copy-start | bytes 276484
  6.4 26.5 %copy-start.11 = (bf16[256,128]{1,0:T(8,128)(2,1)S(1)}, bf16[256,128]{1,0:T(8,128)(2,1)}, u32[]{:S(2)}) copy-start(bf16[256,128]{1,0:T(8,128)(2,1)} %constant.32.clone.w1c) | copy-start | bytes 196612

commit v2 on v1

v2 whole, which is shorter than its diff:
```python
import functools

import jax
import jax.numpy as jnp
import ml_dtypes
import numpy as np
from jax import lax
from jax.experimental import pallas as pl
from jax.experimental.pallas import tpu as pltpu
from jax.sharding import PartitionSpec as P

predict_one = -1.586134342
update_one = -0.05298011854
predict_two = 0.8829110762
update_two = 0.4435068522
scale_factor = 1.149604398

MESH = pl.DeviceIdType.MESH
F32 = jnp.float32
BF16 = jnp.bfloat16
NX, HX = 128, 64
BY, BZ = 64, 128
LOW_ROWS, HIGH_ROWS = 4 * HX, 2 * HX


def lift_rows(v):
    s, d = v[0::2], v[1::2]
    d = d + predict_one * (s + np.roll(s, -1, 0))
    s = s + update_one * (np.roll(d, 1, 0) + d)
    d = d + predict_two * (s + np.roll(s, -1, 0))
    s = s + update_two * (np.roll(d, 1, 0) + d)
    return s * scale_factor, d / scale_factor


def factored(block, fine):
    first = np.linalg.svd(block[:fine])[2][:2]
    rest = block[fine:] - (block[fine:] @ first.T) @ first
    second = np.linalg.svd(rest)[2][:2]
    basis = np.concatenate([first, second])
    gains = block @ basis.T
    gains[:fine, 2:] = 0
    return basis, gains


@functools.cache
def operators(n):
    low, high = lift_rows(np.eye(3 * n))
    low2, high2 = lift_rows(low)
    h, q = n // 2, n // 4
    rows = np.concatenate([low[h : 2 * h], high[h : 2 * h], low2[q : 2 * q], high2[q : 2 * q]])
    return rows[:, n : 2 * n], factored(rows[:, :n], n), factored(rows[:, 2 * n :], n)


def halves(w):
    hi = w.astype(ml_dtypes.bfloat16)
    return hi, (w - hi.astype(np.float64)).astype(ml_dtypes.bfloat16)


def three(w, axis):
    hi, lo = halves(w)
    return np.concatenate([hi, hi, lo], axis)


@functools.cache
def constants():
    own_y, (basis_left, gain_left), (basis_right, gain_right) = operators(BY)
    y_low = np.zeros((2, 96, 80))
    y_high = np.zeros((4, 64, 80))
    for p in range(2):
        y_low[p, :, :64] = own_y
        y_low[p, :, 64 + 4 * p : 68 + 4 * p] = gain_left
        y_low[p, :, 72 + 4 * p : 76 + 4 * p] = gain_right
    for p in range(4):
        y_high[p, :, :64] = own_y[:64]
        y_high[p, :, 64 + 2 * p : 66 + 2 * p] = gain_left[:64, :2]
        y_high[p, :, 72 + 2 * p : 74 + 2 * p] = gain_right[:64, :2]
    edge = np.r_[0:16, 48:64]
    assert abs(np.delete(basis_left, edge, 1)).max() < 1e-12
    assert abs(np.delete(basis_right, edge, 1)).max() < 1e-12
    state_low = np.zeros((64, 256))
    state_high = np.zeros((32, 256))
    for side, basis in enumerate((basis_right, basis_left)):
        for i in range(8):
            columns = slice(32 * i, 32 * i + 32)
            state_low[32 * side + 4 * i : 32 * side + 4 * i + 4, columns] = basis[:, edge]
            state_high[16 * side + 2 * i : 16 * side + 2 * i + 2, columns] = basis[:2, edge]

    own_z, (left, gain_l), (right, gain_r) = operators(BZ)
    zs_low = np.concatenate([np.tile(b.T, (1, 16)) for b in (right, left)], 1)
    zs_high = np.concatenate([np.tile(b[:2].T, (1, 32)) for b in (right, left)], 1)

    def spread(rows):
        k = rows.shape[1]
        fine = np.zeros((k, 256))
        fine[:, :64] = rows[:64].T
        fine[:, 128:192] = rows[64:128].T
        coarse = np.zeros((k, 128))
        coarse[:, :64] = rows[128:].T
        return fine, coarse

    main_fine, main_coarse = spread(own_z)
    halo_fine, halo_coarse = spread(np.concatenate([gain_l, gain_r], 1))

    def passes(main, halo):
        hi, lo = halves(main)
        ehi, elo = halves(halo)
        table = np.zeros((4, 512, main.shape[1]), ml_dtypes.bfloat16)
        for i in range(4):
            table[i, :384] = np.concatenate([hi, hi, lo], 0)
            table[i, 384 + 32 * i : 384 + 32 * i + 24] = np.concatenate([ehi, ehi, elo], 0)
        return table

    def places(states):
        p = np.zeros((4, 128, 128))
        for lane in range(128):
            i, s = lane // states % 4, lane % states
            p[0, lane, 32 * i + s] = p[0, lane, 32 * i + 16 + s] = 1
            p[1, lane, 32 * i + 8 + s] = 1
            p[2, lane, 32 * i + 4 + s] = p[2, lane, 32 * i + 20 + s] = 1
            p[3, lane, 32 * i + 12 + s] = 1
        return p.reshape(512, 128).astype(ml_dtypes.bfloat16)

    wf, wc = passes(main_fine, halo_fine), passes(main_coarse, halo_coarse)
    y_low, y_high = three(y_low, 2), three(y_high, 2)
    send = (three(state_low, 1), three(state_high, 1), three(zs_low, 0), three(zs_high, 0), y_low, y_high)
    work = (y_low, wf, wc, places(4), places(2))
    return send, work


def split(v):
    hi = v.astype(BF16)
    return hi, (v - hi.astype(F32)).astype(BF16)


def dot(a, b):
    return jnp.dot(a, b, preferred_element_type=F32)


def lift_loop(count, unroll, load, store):
    k = 2 * count
    s_a, d_a, s_b, d_b, s_c, d_c, s_d = [load(i % k) for i in range(k - 4, k + 3)]
    d_a = d_a + predict_one * (s_a + s_b)
    d_b = d_b + predict_one * (s_b + s_c)
    s_b = s_b + update_one * (d_a + d_b)
    d_c = d_c + predict_one * (s_c + s_d)
    s_c = s_c + update_one * (d_b + d_c)
    d_b = d_b + predict_two * (s_b + s_c)

    def step(j, carry):
        s_now, d_before, s_before, d_done = carry
        for u in range(unroll):
            n = unroll * j + u + 1
            d_now, s_next = load(lax.rem(2 * n + 1, k)), load(lax.rem(2 * n + 2, k))
            d_now = d_now + predict_one * (s_now + s_next)
            s_now = s_now + update_one * (d_before + d_now)
            d_before = d_before + predict_two * (s_before + s_now)
            s_before = s_before + update_two * (d_done + d_before)
            store(n - 1, s_before * scale_factor, d_before * (1.0 / scale_factor))
            s_now, d_before, s_before, d_done = s_next, d_now, s_now, d_before
        return s_now, d_before, s_before, d_done

    lax.fori_loop(0, count // unroll, step, (s_d, d_c, s_c, d_b))


def lift_x(v, x_hi, x_lo, rows):
    def store(n, low, high):
        x_hi[n, rows], x_lo[n, rows] = split(low)
        x_hi[HX + n, rows], x_lo[HX + n, rows] = split(high)

    lift_loop(HX, 4, lambda i: v[i, rows], store)


def find_y_states(x_hi, x_lo, st_low, st_high, y_send):
    for half, table, per in ((0, st_low, 4), (1, st_high, 2)):
        n = 8 * per
        for g in range(0, 8, 2):
            columns = []
            for u in (g, g + 1):
                parts = []
                for ref in (x_hi, x_lo):
                    for x in range(HX * half + 8 * u, HX * half + 8 * u + 8):
                        parts += [ref[x, 0:16], ref[x, 48:64]]
                columns.append(jnp.concatenate(parts + parts[:16], 0))
            states = dot(table[...], jnp.concatenate(columns, 1))
            for u in (0, 1):
                at = LOW_ROWS * half + n * (g + u)
                for side in (0, 1):
                    piece = states[n * side : n * side + n, 128 * u : 128 * u + 128]
                    y_send[side, at : at + n] = piece


def find_z_states(x_hi, x_lo, zs_low, zs_high, z_send):
    lane = lax.broadcasted_iota(jnp.int32, (8, 128), 1)
    lower = (lane < 64)[None]
    for group, (first, count, table, per) in enumerate(
        ((0, 32, zs_low, 4), (32, 32, zs_low, 4), (64, 64, zs_high, 2))
    ):
        slot = lane % 64 // per
        n = count // 2
        both = []
        for at in (first, first + n):
            hi = x_hi[at : at + n].reshape(n * BY, BZ)
            lo = x_lo[at : at + n].reshape(n * BY, BZ)
            states = dot(jnp.concatenate([hi, lo, hi], 1), table[...]).reshape(n, 8, 8, 128)
            acc = states[0]
            for i in range(1, n):
                acc = jnp.where((slot == i)[None], states[i], acc)
            both.append(acc)
        one, two = both
        rows = slice(64 * group, 64 * group + 64)
        z_send[0, rows] = jnp.where(lower, one, pltpu.roll(two, 64, 2)).reshape(64, 128)
        z_send[1, rows] = jnp.where(lower, pltpu.roll(one, 64, 2), two).reshape(64, 128)


def find_corners(z_send, st_low, c_send):
    his, los = [], []
    zeros = jnp.zeros((32, 128), F32)
    for side in range(2):
        for group in range(4):
            if group == 3:
                piece = zeros
            else:
                at = 64 * group
                piece = jnp.concatenate(
                    [z_send[side, at : at + 16], z_send[side, at + 48 : at + 64]], 0
                )
            hi, lo = split(piece)
            his.append(hi)
            los.append(lo)
    c_send[...] = dot(st_low[...], jnp.concatenate(his + los + his, 0)).reshape(4, 16, 128)


STEPS = [(-1, 0), (1, 0), (0, -1), (0, 1), (-1, -1), (-1, 1), (1, -1), (1, 1)]
ORDER = (0, 3, 1, 2)


def exchange_kernel(
    v_hbm, st_low_hbm, st_high_hbm, zs_low_hbm, zs_high_hbm, y_low_hbm, y_high_hbm,
    lhs_low, lhs_high, z_recv, c_recv,
    v, x_hi, x_lo, y_send, z_send, c_send, y_recv,
    st_low, st_high, zs_low, zs_high, y_low, y_high, in_sem, send_sem, recv_sem,
):
    my_y, my_z = lax.axis_index("gy"), lax.axis_index("gz")
    n_y, n_z = lax.axis_size("gy"), lax.axis_size("gz")

    def device(step_y, step_z):
        return {
            "gy": lax.rem(my_y + step_y + n_y, n_y),
            "gz": lax.rem(my_z + step_z + n_z, n_z),
        }

    barrier = pltpu.get_barrier_semaphore()
    for step in STEPS:
        pl.semaphore_signal(barrier, inc=1, device_id=device(*step), device_id_type=MESH)

    def load(k, src, dst):
        copy = pltpu.make_async_copy(src, dst, in_sem.at[k])
        copy.start()
        return copy

    def load_rows(c):
        rows = pl.ds(16 * c, 16)
        return load(c, v_hbm.at[:, rows], v.at[:, rows])

    loads = {c: load_rows(c) for c in ORDER[:2]}
    loads[4] = load(4, st_low_hbm, st_low)
    loads[5] = load(5, st_high_hbm, st_high)
    loads.update({c: load_rows(c) for c in ORDER[2:]})
    loads[6] = load(6, zs_low_hbm, zs_low)
    loads[7] = load(7, zs_high_hbm, zs_high)
    loads[8] = load(8, y_low_hbm, y_low)
    loads[9] = load(9, y_high_hbm, y_high)

    def lift(c):
        loads[c].wait()
        lift_x(v, x_hi, x_lo, pl.ds(16 * c, 16))

    def send(k):
        source = (y_send, z_send, c_send)[k // 2 if k < 4 else 2]
        target = (y_recv, z_recv, c_recv)[k // 2 if k < 4 else 2]
        at, to = (k % 2, 1 - k % 2) if k < 4 else (k - 4, 7 - k)
        copy = pltpu.make_async_remote_copy(
            src_ref=source.at[at], dst_ref=target.at[to],
            send_sem=send_sem.at[k], recv_sem=recv_sem.at[k],
            device_id=device(*STEPS[k]), device_id_type=MESH,
        )
        copy.start()
        return copy

    lift(ORDER[0])
    lift(ORDER[1])
    loads[4].wait()
    loads[5].wait()
    find_y_states(x_hi, x_lo, st_low, st_high, y_send)
    pl.semaphore_wait(barrier, 8)
    y_copies = [send(k) for k in (0, 1)]

    lift(ORDER[2])
    lift(ORDER[3])
    loads[6].wait()
    loads[7].wait()
    find_z_states(x_hi, x_lo, zs_low, zs_high, z_send)
    z_copies = [send(k) for k in (2, 3)]
    find_corners(z_send, st_low, c_send)
    z_copies += [send(k) for k in range(4, 8)]

    loads[8].wait()
    loads[9].wait()
    for copy in y_copies:
        copy.wait()
    for part in range(4):
        lift_y(part, True, x_hi, x_lo, y_recv, y_low, lhs_low)
        lift_y(part, False, x_hi, x_lo, y_recv, y_high, lhs_high)
    for copy in z_copies:
        copy.wait()


def stacked(hi, lo, tiles):
    thi, tlo = split(tiles)
    return jnp.concatenate([hi, thi, lo, tlo, hi, thi], 0)


def lift_z_halos(z_recv, c_recv, y_low, p_low, p_high, zh_low, zh_high):
    lane = lax.broadcasted_iota(jnp.int32, (1, 512), 1) % 128
    for group in range(3):
        blocks = []
        for side in range(2):
            hi, lo = split(z_recv[side, 64 * group : 64 * group + 64])
            at = 8 * (group // 2)
            tiles = jnp.concatenate([c_recv[side, at : at + 8], c_recv[2 + side, at : at + 8]], 0)
            blocks += split(dot(y_low[group % 2], stacked(hi, lo, tiles)))
        both = jnp.concatenate(blocks, 1)
        if group < 2:
            masked = [both * jnp.where(lane // 16 == g, 1.0, 0.0).astype(BF16) for g in range(8)]
            placed = dot(jnp.concatenate(masked, 0), p_low[...]).astype(BF16)
            zh_low[8 * group : 8 * group + 8] = placed.reshape(8, 96, 128)
        else:
            both = both[:64]
            masked = [both * jnp.where(lane // 8 == g, 1.0, 0.0).astype(BF16) for g in range(16)]
            placed = dot(jnp.concatenate(masked, 0), p_high[...]).astype(BF16)
            zh_high[...] = placed.reshape(16, 64, 128)


def lift_y(part, low, x_hi, x_lo, y_recv, table, lhs):
    first = 0 if low else HX
    for i in range(4):
        for q in range(0, 4, 2):
            columns = []
            for u in (q, q + 1):
                x = 16 * part + 4 * u + i
                at = 8 * (x // 2) if low else LOW_ROWS + 8 * (x // 4)
                tiles = jnp.concatenate([y_recv[0, at : at + 8], y_recv[1, at : at + 8]], 0)
                columns.append(stacked(x_hi[first + x], x_lo[first + x], tiles))
            which = i % 2 if low else i
            hi, lo = split(dot(table[which], jnp.concatenate(columns, 1)))
            for u in (0, 1):
                lhs[0, part, i, q + u] = hi[:, 128 * u : 128 * u + 128]
                lhs[1, part, i, q + u] = lo[:, 128 * u : 128 * u + 128]


def lift_z(part, i, zh, lhs, table, start, rows):
    hi = lhs[0, part, i, :, start : start + rows].reshape(4 * rows, 128)
    lo = lhs[1, part, i, :, start : start + rows].reshape(4 * rows, 128)
    zh = zh[4 * part : 4 * part + 4, start : start + rows].reshape(4 * rows, 128)
    return dot(jnp.concatenate([hi, lo, hi, zh], 1), table[i])


def low_part(part, lhs, zh_low, wf, wc, fine, level):
    for i in range(4):
        one = lift_z(part, i, zh_low, lhs, wf, 0, 64)
        two = lift_z(part, i, zh_low, lhs, wc, 64, 32)
        for q in range(4):
            x = 16 * part + 4 * q + i
            fine[0, x] = one[64 * q : 64 * q + 32, 128:192]
            fine[1, x] = one[64 * q + 32 : 64 * q + 64, :64]
            fine[2, x] = one[64 * q + 32 : 64 * q + 64, 128:192]
            level[x] = two[32 * q : 32 * q + 32]


def high_part(part, lhs, zh_high, wf, fine):
    for i in range(4):
        one = lift_z(part, i, zh_high, lhs, wf, 0, 64)
        for q in range(4):
            x = 16 * part + 4 * q + i
            fine[3, x] = one[64 * q : 64 * q + 32, :64]
            fine[4, x] = one[64 * q : 64 * q + 32, 128:192]
            fine[5, x] = one[64 * q + 32 : 64 * q + 64, :64]
            fine[6, x] = one[64 * q + 32 : 64 * q + 64, 128:192]


def lift_level(level, coarse):
    def store(n, low, high):
        for bx, value in enumerate((low, high)):
            for by in range(2):
                for bz in range(2):
                    coarse[4 * bx + 2 * by + bz, n] = value[
                        16 * by : 16 * by + 16, 32 * bz : 32 * bz + 32
                    ]

    lift_loop(HX // 2, 8, lambda i: level[i], store)


def finish_kernel(
    lhs_low, lhs_high, z_recv, c_recv, y_low, wf, wc, p_low, p_high,
    fine_hbm, coarse_hbm,
    fine, coarse, level, zh_low, zh_high, sem,
):
    lift_z_halos(z_recv, c_recv, y_low, p_low, p_high, zh_low, zh_high)
    copies = []

    def write(bands, part):
        at = pl.ds(16 * part, 16)
        src, dst = fine.at[pl.ds(*bands), at], fine_hbm.at[pl.ds(*bands), at]
        copies.append(pltpu.make_async_copy(src, dst, sem.at[part + (4 if bands == HIGH_BANDS else 0)]))
        copies[-1].start()

    for part in range(4):
        low_part(part, lhs_low, zh_low, wf, wc, fine, level)
        write(LOW_BANDS, part)
    lift_level(level, coarse)
    copies.append(pltpu.make_async_copy(coarse, coarse_hbm, sem.at[8]))
    copies[-1].start()
    for part in range(4):
        high_part(part, lhs_high, zh_high, wf, fine)
        write(HIGH_BANDS, part)
    for copy in copies:
        copy.wait()


LOW_BANDS, HIGH_BANDS = (0, 3), (3, 4)


def body(velocity):
    send, work = constants()
    vmem = pl.BlockSpec(memory_space=pltpu.VMEM)
    hbm = pl.BlockSpec(memory_space=pltpu.HBM)
    shape = jax.ShapeDtypeStruct
    y_shape, z_shape, c_shape = (2, LOW_ROWS + HIGH_ROWS, BZ), (2, 3 * BY, 128), (4, 16, 128)
    halos = pl.pallas_call(
        exchange_kernel,
        out_shape=(
            shape((2, 4, 4, 4, 96, 128), BF16), shape((2, 4, 4, 4, 64, 128), BF16),
            shape(z_shape, F32), shape(c_shape, F32),
        ),
        in_specs=[hbm] * 7,
        out_specs=(vmem,) * 4,
        scratch_shapes=[
            pltpu.VMEM((NX, BY, BZ), F32),
            pltpu.VMEM((NX, BY, BZ), BF16),
            pltpu.VMEM((NX, BY, BZ), BF16),
            pltpu.VMEM(y_shape, F32),
            pltpu.VMEM(z_shape, F32),
            pltpu.VMEM(c_shape, F32),
            pltpu.VMEM(y_shape, F32),
            *[pltpu.VMEM(a.shape, BF16) for a in send],
            pltpu.SemaphoreType.DMA((10,)),
            pltpu.SemaphoreType.DMA((8,)),
            pltpu.SemaphoreType.DMA((8,)),
        ],
        compiler_params=pltpu.CompilerParams(
            collective_id=0, has_side_effects=True, vmem_limit_bytes=32 * 2**20
        ),
        name="exchange",
    )(*[pltpu.with_memory_space_constraint(jnp.asarray(a), pltpu.HBM) for a in (velocity, *send)])
    fine_shape, coarse_shape = (7, HX, BY // 2, BZ // 2), (8, HX // 2, BY // 4, BZ // 4)
    return pl.pallas_call(
        finish_kernel,
        out_shape=(shape(fine_shape, F32), shape(coarse_shape, F32)),
        in_specs=[vmem] * 9,
        out_specs=(hbm, hbm),
        scratch_shapes=[
            pltpu.VMEM(fine_shape, F32),
            pltpu.VMEM(coarse_shape, F32),
            pltpu.VMEM((HX, 32, 128), F32),
            pltpu.VMEM((16, 96, 128), BF16),
            pltpu.VMEM((16, 64, 128), BF16),
            pltpu.SemaphoreType.DMA((9,)),
        ],
        compiler_params=pltpu.CompilerParams(vmem_limit_bytes=28 * 2**20),
        name="finish",
    )(*halos, *[jnp.asarray(a) for a in work])


def solution(mesh):
    return jax.shard_map(
        body,
        mesh=mesh,
        in_specs=(P(None, "gy", "gz"),),
        out_specs=(P(None, None, "gy", "gz"), P(None, None, "gy", "gz")),
        check_vma=False,
    )
```

time: 59.6 us -> 26.6 us (0.45)
  Pallas kernels: 52.8 us -> 25.7 us
  local copies, waits for them, and re-layouts: 5.77 us -> 0.03 us
    pallas_call x1, Pallas kernels: 26.4 us -> 6.07 us  [body(): pl.pallas_call(finish_kernel, out_shape=(shape(fine_shape, F32), shape(co...]
    pallas_call x1, Pallas kernels: 26.4 us -> 19.7 us  [body(): pl.pallas_call(exchange_kernel, out_shape=(shape((2, 4, 4, 4, 96, 128), B...]
    unnamed x26 -> x10, local copies, waits for them, and re-layouts: 5.77 us -> 0.03 us
where the time goes in v2:
time: 26.6 us; the launch traced here: 26.5 us
  Pallas kernels  25.7 us (97%)
  between operations  0.72 us (3%)
    pallas_call x1, Pallas kernels, body(): pl.pallas_call(exchange_kernel, out_shape=(shape((2, 4, 4, 4, 96, 128), B...  19.7 us
    pallas_call x1, Pallas kernels, body(): pl.pallas_call(finish_kernel, out_shape=(shape(fine_shape, F32), shape(co...  6.07 us

profile of v2, /device:TPU:1, one launch (start us, length us, event | category | flops | bytes accessed | tf_op | source)
XLA Modules:
  0.0 26.5 jit_solution(12591019753486501708)
XLA Ops:
  0.6 0.0 copy-start.2
  0.6 0.0 copy-start.3
  0.7 0.0 copy-start.4
  0.7 0.0 copy-start.1
  0.7 0.0 copy-start
  0.7 19.7 %exchange.1 = (bf16[2,4,4,4,96,128]{5,4,3,2,1,0:T(8,128)(2,1)S(1)}, bf16[2,4,4,4,64,128]{5,4,3,2,1,0:T(8,128)(2,1)S(1)}, f32[2,192,128]{2,1,0:T(8,128)S(1)}, f32[4,16,128]{2,1,0:T(8,128)S(1)}) custom-call(f32[128,64,128]{2,1,0:T(8,128)} %v_hbm.1, bf16[64,768]{1,0:T(8,128)(2,1)} %constant.20.clone.st_low_hbm, bf16[32,768]{1,0:T(8,128)(2,1)} %constant.21.clone.st_high_hbm, ...), custom_call_target="tpu_custom_call" | custom-call | tf_op jit(solution)/shard_map/exchange/pallas_call | solution.py:439
  20.4 0.0 copy-done.2
  20.4 0.0 copy-done.3
  20.4 0.0 copy-done.4
  20.4 0.0 copy-done.1
  20.4 0.0 copy-done
  20.4 6.1 %finish.1 = (f32[7,64,32,64]{3,2,1,0:T(8,128)}, f32[8,32,16,32]{3,2,1,0:T(8,128)}) custom-call(bf16[2,4,4,4,96,128]{5,4,3,2,1,0:T(8,128)(2,1)S(1)} %get-tuple-element.6.lhs_low, bf16[2,4,4,4,64,128]{5,4,3,2,1,0:T(8,128)(2,1)S(1)} %get-tuple-element.7.lhs_high, f32[2,192,128]{2,1,0:T(8,128)S(1)} %get-tuple-element.8.z_recv, ...), custom_call_target="tpu_custom_call" | custom-call | tf_op jit(solution)/shard_map/finish/pallas_call | solution.py:466
Async XLA Ops:
  0.6 19.7 %copy-start.2 = (bf16[2,96,240]{2,1,0:T(8,128)(2,1)S(1)}, bf16[2,96,240]{2,1,0:T(8,128)(2,1)}, u32[]{:S(2)}) copy-start(bf16[2,96,240]{2,1,0:T(8,128)(2,1)} %constant.24.clone.y_low_hbm.y_low) | copy-start | bytes 276484
  0.6 19.7 %copy-start.3 = (bf16[512,128]{1,0:T(8,128)(2,1)S(1)}, bf16[512,128]{1,0:T(8,128)(2,1)}, u32[]{:S(2)}) copy-start(bf16[512,128]{1,0:T(8,128)(2,1)} %constant.29.clone.p_high) | copy-start | bytes 393220
  0.7 19.7 %copy-start.4 = (bf16[512,128]{1,0:T(8,128)(2,1)S(1)}, bf16[512,128]{1,0:T(8,128)(2,1)}, u32[]{:S(2)}) copy-start(bf16[512,128]{1,0:T(8,128)(2,1)} %constant.28.clone.p_low) | copy-start | bytes 393220
  0.7 19.7 %copy-start.1 = (bf16[4,512,128]{2,1,0:T(8,128)(2,1)S(1)}, bf16[4,512,128]{2,1,0:T(8,128)(2,1)}, u32[]{:S(2)}) copy-start(bf16[4,512,128]{2,1,0:T(8,128)(2,1)} %constant.27.clone.wc) | copy-start | bytes 1572868
  0.7 19.7 %copy-start = (bf16[4,512,256]{2,1,0:T(8,128)(2,1)S(1)}, bf16[4,512,256]{2,1,0:T(8,128)(2,1)}, u32[]{:S(2)}) copy-start(bf16[4,512,256]{2,1,0:T(8,128)(2,1)} %constant.26.clone.wf) | copy-start | bytes 3145732

commit v3 on v2

--- a/solution.py
+++ b/solution.py
@@ -20,7 +20,8 @@
 BF16 = jnp.bfloat16
 NX, HX = 128, 64
 BY, BZ = 64, 128
-LOW_ROWS, HIGH_ROWS = 4 * HX, 2 * HX
+Y_ROWS = 2 * NX + HX
+Z_ROWS = 2 * BY + BY // 2
 
 
 def lift_rows(v):
@@ -64,16 +65,25 @@
 @functools.cache
 def constants():
     own_y, (basis_left, gain_left), (basis_right, gain_right) = operators(BY)
-    y_low = np.zeros((2, 96, 80))
-    y_high = np.zeros((4, 64, 80))
-    for p in range(2):
+    y_low = np.zeros((4, 96, 80))
+    for p in range(4):
         y_low[p, :, :64] = own_y
-        y_low[p, :, 64 + 4 * p : 68 + 4 * p] = gain_left
-        y_low[p, :, 72 + 4 * p : 76 + 4 * p] = gain_right
+        y_low[p, :, 64 + 2 * p : 66 + 2 * p] = gain_left[:, :2]
+        y_low[p, :, 72 + 2 * p : 74 + 2 * p] = gain_right[:, :2]
+    y_high = y_low[:, :64]
+    y_more = np.zeros((4, 32, 16))
     for p in range(4):
-        y_high[p, :, :64] = own_y[:64]
-        y_high[p, :, 64 + 2 * p : 66 + 2 * p] = gain_left[:64, :2]
-        y_high[p, :, 72 + 2 * p : 74 + 2 * p] = gain_right[:64, :2]
+        y_more[p, :, 2 * p : 2 * p + 2] = gain_left[64:, 2:]
+        y_more[p, :, 8 + 2 * p : 10 + 2 * p] = gain_right[64:, 2:]
+    corner = np.zeros((2, 96, 32))
+    for group in range(2):
+        for side, gain in enumerate((gain_left, gain_right)):
+            for p in range(2):
+                at = 16 * p + 8 * side + 2 * group
+                corner[group, :, at : at + 2] = gain[:, 2 * p : 2 * p + 2]
+    z_one = np.concatenate([own_y, corner[0]], 1)
+    z_two = corner[1, 64:]
+    coarse_y = own_y[64:]
     edge = np.r_[0:16, 48:64]
     assert abs(np.delete(basis_left, edge, 1)).max() < 1e-12
     assert abs(np.delete(basis_right, edge, 1)).max() < 1e-12
@@ -82,12 +92,18 @@
     for side, basis in enumerate((basis_right, basis_left)):
         for i in range(8):
             columns = slice(32 * i, 32 * i + 32)
-            state_low[32 * side + 4 * i : 32 * side + 4 * i + 4, columns] = basis[:, edge]
+            for p in range(2):
+                at = 32 * side + 16 * p + 2 * i
+                state_low[at : at + 2, columns] = basis[2 * p : 2 * p + 2, edge]
             state_high[16 * side + 2 * i : 16 * side + 2 * i + 2, columns] = basis[:2, edge]
 
     own_z, (left, gain_l), (right, gain_r) = operators(BZ)
-    zs_low = np.concatenate([np.tile(b.T, (1, 16)) for b in (right, left)], 1)
+    zs_low = np.concatenate([np.tile(b[p : p + 2].T, (1, 16)) for b in (right, left) for p in (0, 2)], 1)
     zs_high = np.concatenate([np.tile(b[:2].T, (1, 32)) for b in (right, left)], 1)
+    coarse_z = np.zeros((2, 384, 128), ml_dtypes.bfloat16)
+    for p in range(2):
+        coarse_z[p, :, 64 * p : 64 * p + 64] = three(own_z[128:].T, 0)
+    coarse_z = coarse_z.reshape(768, 128)
 
     def spread(rows):
         k = rows.shape[1]
@@ -110,10 +126,10 @@
             table[i, 384 + 32 * i : 384 + 32 * i + 24] = np.concatenate([ehi, ehi, elo], 0)
         return table
 
-    def places(states):
+    def places(first):
         p = np.zeros((4, 128, 128))
         for lane in range(128):
-            i, s = lane // states % 4, lane % states
+            i, s = lane // 2 % 4, first + lane % 2
             p[0, lane, 32 * i + s] = p[0, lane, 32 * i + 16 + s] = 1
             p[1, lane, 32 * i + 8 + s] = 1
             p[2, lane, 32 * i + 4 + s] = p[2, lane, 32 * i + 20 + s] = 1
@@ -121,9 +137,14 @@
         return p.reshape(512, 128).astype(ml_dtypes.bfloat16)
 
     wf, wc = passes(main_fine, halo_fine), passes(main_coarse, halo_coarse)
-    y_low, y_high = three(y_low, 2), three(y_high, 2)
-    send = (three(state_low, 1), three(state_high, 1), three(zs_low, 0), three(zs_high, 0), y_low, y_high)
-    work = (y_low, wf, wc, places(4), places(2))
+    send = (
+        three(state_low, 1), three(state_high, 1), three(zs_low, 0), three(zs_high, 0), coarse_z, three(coarse_y, 1),
+        three(y_low, 2), three(y_high, 2), three(y_more, 2).reshape(128, 48),
+    )
+    work = (
+        three(z_one, 1), three(z_two, 1), three(y_high[2], 1), wf, wc,
+        np.concatenate([places(0), places(2)], 0),
+    )
     return send, work
 
 
@@ -167,12 +188,13 @@
         x_hi[n, rows], x_lo[n, rows] = split(low)
         x_hi[HX + n, rows], x_lo[HX + n, rows] = split(high)
 
-    lift_loop(HX, 4, lambda i: v[i, rows], store)
-
-
-def find_y_states(x_hi, x_lo, st_low, st_high, y_send):
-    for half, table, per in ((0, st_low, 4), (1, st_high, 2)):
-        n = 8 * per
+    lift_loop(HX, 16, lambda i: v[i, rows], store)
+
+
+def find_y_states(x_hi, x_lo, st_low, st_high, coarse_z, y_send):
+    more = [[], []]
+    for half, table in ((0, st_low), (1, st_high)):
+        n = 16
         for g in range(0, 8, 2):
             columns = []
             for u in (g, g + 1):
@@ -183,51 +205,77 @@
                 columns.append(jnp.concatenate(parts + parts[:16], 0))
             states = dot(table[...], jnp.concatenate(columns, 1))
             for u in (0, 1):
-                at = LOW_ROWS * half + n * (g + u)
+                at = NX * half + n * (g + u)
                 for side in (0, 1):
-                    piece = states[n * side : n * side + n, 128 * u : 128 * u + 128]
-                    y_send[side, at : at + n] = piece
-
-
-def find_z_states(x_hi, x_lo, zs_low, zs_high, z_send):
+                    first = (n if half else 2 * n) * side
+                    lanes = slice(128 * u, 128 * u + 128)
+                    y_send[side, at : at + n] = states[first : first + n, lanes]
+                    if not half:
+                        more[side].append(states[first + n : first + 2 * n, lanes])
+    pieces = []
+    for part in range(2):
+        hi, lo = split(jnp.concatenate(more[0][4 * part : 4 * part + 4] + more[1][4 * part : 4 * part + 4], 0))
+        pieces += [hi, lo, hi]
+    lifted = dot(jnp.concatenate(pieces, 1), coarse_z[...])
+    y_send[0, 2 * NX :] = lifted[:HX]
+    y_send[1, 2 * NX :] = lifted[HX:]
+
+
+def find_z_states(x_hi, x_lo, zs_low, zs_high, coarse_y, z_send, z_raw):
     lane = lax.broadcasted_iota(jnp.int32, (8, 128), 1)
-    lower = (lane < 64)[None]
-    for group, (first, count, table, per) in enumerate(
-        ((0, 32, zs_low, 4), (32, 32, zs_low, 4), (64, 64, zs_high, 2))
-    ):
-        slot = lane % 64 // per
-        n = count // 2
-        both = []
-        for at in (first, first + n):
-            hi = x_hi[at : at + n].reshape(n * BY, BZ)
-            lo = x_lo[at : at + n].reshape(n * BY, BZ)
-            states = dot(jnp.concatenate([hi, lo, hi], 1), table[...]).reshape(n, 8, 8, 128)
-            acc = states[0]
-            for i in range(1, n):
-                acc = jnp.where((slot == i)[None], states[i], acc)
-            both.append(acc)
-        one, two = both
-        rows = slice(64 * group, 64 * group + 64)
-        z_send[0, rows] = jnp.where(lower, one, pltpu.roll(two, 64, 2)).reshape(64, 128)
-        z_send[1, rows] = jnp.where(lower, pltpu.roll(one, 64, 2), two).reshape(64, 128)
-
-
-def find_corners(z_send, st_low, c_send):
+
+    def states_of(first, n, table, slot):
+        hi = x_hi[first : first + n].reshape(n * BY, BZ)
+        lo = x_lo[first : first + n].reshape(n * BY, BZ)
+        states = dot(jnp.concatenate([hi, lo, hi], 1), table[...]).reshape(n, 8, 8, 128)
+        acc = states[0]
+        for i in range(1, n):
+            acc = jnp.where((slot == i)[None], states[i], acc)
+        return acc
+
+    def gathered(pieces, of):
+        width = 128 // len(pieces)
+        out = None
+        for k, piece in enumerate(pieces):
+            turn = (width * (k - of)) % 128
+            moved = pltpu.roll(piece, turn, 2) if turn else piece
+            out = moved if out is None else jnp.where((lane // width == k)[None], moved, out)
+        return out.reshape(64, 128)
+
+    low = [states_of(16 * k, 16, zs_low, lane % 32 // 2) for k in range(4)]
+    high = [states_of(HX + 32 * k, 32, zs_high, lane % 64 // 2) for k in range(2)]
+    columns = []
+    for side in range(2):
+        z_send[side, 0:64] = gathered(low, 2 * side)
+        z_send[side, 64:128] = gathered(high, side)
+        second = gathered(low, 2 * side + 1)
+        z_raw[side] = second
+        hi, lo = split(second)
+        columns.append(jnp.concatenate([hi, lo, hi], 0))
+    lifted = dot(coarse_y[...], jnp.concatenate(columns, 1))
+    z_send[0, 128:160] = lifted[:, :128]
+    z_send[1, 128:160] = lifted[:, 128:]
+
+
+def find_corners(z_send, z_raw, st_low, c_send):
     his, los = [], []
     zeros = jnp.zeros((32, 128), F32)
     for side in range(2):
-        for group in range(4):
-            if group == 3:
-                piece = zeros
-            else:
-                at = 64 * group
-                piece = jnp.concatenate(
-                    [z_send[side, at : at + 16], z_send[side, at + 48 : at + 64]], 0
-                )
-            hi, lo = split(piece)
+        for top, low in (
+            (z_send[side, 0:16], z_send[side, 48:64]),
+            (z_raw[side, 0:16], z_raw[side, 48:64]),
+            (z_send[side, 64:80], z_send[side, 112:128]),
+            (zeros[:16], zeros[:16]),
+        ):
+            hi, lo = split(jnp.concatenate([top, low], 0))
             his.append(hi)
             los.append(lo)
-    c_send[...] = dot(st_low[...], jnp.concatenate(his + los + his, 0)).reshape(4, 16, 128)
+    states = dot(st_low[...], jnp.concatenate(his + los + his, 0))
+    for y in range(2):
+        for z in range(2):
+            for p in range(2):
+                at = 32 * y + 16 * p + 8 * z
+                c_send[2 * y + z, 8 * p : 8 * p + 8] = states[at : at + 8]
 
 
 STEPS = [(-1, 0), (1, 0), (0, -1), (0, 1), (-1, -1), (-1, 1), (1, -1), (1, 1)]
@@ -235,10 +283,11 @@
 
 
 def exchange_kernel(
-    v_hbm, st_low_hbm, st_high_hbm, zs_low_hbm, zs_high_hbm, y_low_hbm, y_high_hbm,
-    lhs_low, lhs_high, z_recv, c_recv,
-    v, x_hi, x_lo, y_send, z_send, c_send, y_recv,
-    st_low, st_high, zs_low, zs_high, y_low, y_high, in_sem, send_sem, recv_sem,
+    v_hbm, st_low_hbm, st_high_hbm, zs_low_hbm, zs_high_hbm, coarse_z_hbm, coarse_y_hbm,
+    y_low_hbm, y_high_hbm, y_more_hbm,
+    lhs_low, lhs_high, more, z_recv, c_recv,
+    v, x_hi, x_lo, y_send, z_send, z_raw, c_send, y_recv,
+    st_low, st_high, zs_low, zs_high, coarse_z, coarse_y, y_low, y_high, y_more, in_sem, send_sem, recv_sem,
 ):
     my_y, my_z = lax.axis_index("gy"), lax.axis_index("gz")
     n_y, n_z = lax.axis_size("gy"), lax.axis_size("gz")
@@ -263,13 +312,15 @@
         return load(c, v_hbm.at[:, rows], v.at[:, rows])
 
     loads = {c: load_rows(c) for c in ORDER[:2]}
-    loads[4] = load(4, st_low_hbm, st_low)
-    loads[5] = load(5, st_high_hbm, st_high)
+    tables = [
+        (st_low_hbm, st_low), (st_high_hbm, st_high), (coarse_z_hbm, coarse_z), (zs_low_hbm, zs_low),
+        (zs_high_hbm, zs_high), (coarse_y_hbm, coarse_y), (y_low_hbm, y_low), (y_high_hbm, y_high), (y_more_hbm, y_more),
+    ]
+    for k in (0, 1, 2):
+        loads[4 + k] = load(4 + k, *tables[k])
     loads.update({c: load_rows(c) for c in ORDER[2:]})
-    loads[6] = load(6, zs_low_hbm, zs_low)
-    loads[7] = load(7, zs_high_hbm, zs_high)
-    loads[8] = load(8, y_low_hbm, y_low)
-    loads[9] = load(9, y_high_hbm, y_high)
+    for k in range(3, 9):
+        loads[4 + k] = load(4 + k, *tables[k])
 
     def lift(c):
         loads[c].wait()
@@ -289,25 +340,26 @@
 
     lift(ORDER[0])
     lift(ORDER[1])
-    loads[4].wait()
-    loads[5].wait()
-    find_y_states(x_hi, x_lo, st_low, st_high, y_send)
+    for k in (4, 5, 6):
+        loads[k].wait()
+    find_y_states(x_hi, x_lo, st_low, st_high, coarse_z, y_send)
     pl.semaphore_wait(barrier, 8)
     y_copies = [send(k) for k in (0, 1)]
 
     lift(ORDER[2])
     lift(ORDER[3])
-    loads[6].wait()
-    loads[7].wait()
-    find_z_states(x_hi, x_lo, zs_low, zs_high, z_send)
+    for k in (7, 8, 9):
+        loads[k].wait()
+    find_z_states(x_hi, x_lo, zs_low, zs_high, coarse_y, z_send, z_raw)
     z_copies = [send(k) for k in (2, 3)]
-    find_corners(z_send, st_low, c_send)
+    find_corners(z_send, z_raw, st_low, c_send)
     z_copies += [send(k) for k in range(4, 8)]
 
-    loads[8].wait()
-    loads[9].wait()
+    for k in (10, 11, 12):
+        loads[k].wait()
     for copy in y_copies:
         copy.wait()
+    lift_more(y_recv, y_more, more)
     for part in range(4):
         lift_y(part, True, x_hi, x_lo, y_recv, y_low, lhs_low)
         lift_y(part, False, x_hi, x_lo, y_recv, y_high, lhs_high)
@@ -320,25 +372,45 @@
     return jnp.concatenate([hi, thi, lo, tlo, hi, thi], 0)
 
 
-def lift_z_halos(z_recv, c_recv, y_low, p_low, p_high, zh_low, zh_high):
+def lift_z_halos(z_recv, c_recv, z_one, z_two, z_high, places, zh_low, zh_high):
     lane = lax.broadcasted_iota(jnp.int32, (1, 512), 1) % 128
-    for group in range(3):
-        blocks = []
-        for side in range(2):
-            hi, lo = split(z_recv[side, 64 * group : 64 * group + 64])
-            at = 8 * (group // 2)
-            tiles = jnp.concatenate([c_recv[side, at : at + 8], c_recv[2 + side, at : at + 8]], 0)
-            blocks += split(dot(y_low[group % 2], stacked(hi, lo, tiles)))
-        both = jnp.concatenate(blocks, 1)
-        if group < 2:
-            masked = [both * jnp.where(lane // 16 == g, 1.0, 0.0).astype(BF16) for g in range(8)]
-            placed = dot(jnp.concatenate(masked, 0), p_low[...]).astype(BF16)
-            zh_low[8 * group : 8 * group + 8] = placed.reshape(8, 96, 128)
-        else:
-            both = both[:64]
-            masked = [both * jnp.where(lane // 8 == g, 1.0, 0.0).astype(BF16) for g in range(16)]
-            placed = dot(jnp.concatenate(masked, 0), p_high[...]).astype(BF16)
-            zh_high[...] = placed.reshape(16, 64, 128)
+    masks = [jnp.where(lane // 8 == g, 1.0, 0.0).astype(BF16) for g in range(16)]
+    first, second, high = [], [], []
+    for side in range(2):
+        corners = [c_recv[2 * y + side, 8 * p : 8 * p + 8] for p in range(2) for y in range(2)]
+        tiles = jnp.concatenate(corners, 0)
+        own = z_recv[side]
+        first += split(dot(z_one[...], tripled(jnp.concatenate([own[:64], tiles], 0))))
+        second += split(own[128:160] + dot(z_two[...], tripled(tiles)))
+        high += split(dot(z_high[...], tripled(jnp.concatenate([own[64:128], tiles[:16]], 0))))
+    first, second, high = (jnp.concatenate(blocks, 1) for blocks in (first, second, high))
+    one = jnp.concatenate([high * m for m in masks], 0)
+    zh_high[...] = dot(one, places[:512]).astype(BF16).reshape(16, 64, 128)
+    one = jnp.concatenate([first[:64] * m for m in masks], 0)
+    zh_low[:, :64] = dot(one, places[:512]).astype(BF16).reshape(16, 64, 128)
+    both = [jnp.concatenate([first[64:] * m, second * m], 1) for m in masks]
+    both = dot(jnp.concatenate(both, 0), places[...])
+    zh_low[:, 64:] = both.astype(BF16).reshape(16, 32, 128)
+
+
+def tripled(v):
+    hi, lo = split(v)
+    return jnp.concatenate([hi, lo, hi], 0)
+
+
+def lift_more(y_recv, y_more, more):
+    for t in range(0, 8, 2):
+        columns = []
+        for u in (t, t + 1):
+            at = 2 * NX + 8 * u
+            columns.append(tripled(jnp.concatenate([y_recv[0, at : at + 8], y_recv[1, at : at + 8]], 0)))
+        lifted = dot(y_more[...], jnp.concatenate(columns, 1))
+        for u in (0, 1):
+            for i in range(4):
+                value = lifted[32 * i : 32 * i + 32, 128 * u : 128 * u + 128]
+                x = 4 * (t + u) + i
+                more[x] = value
+                more[HX // 2 + x] = pltpu.roll(value, 64, 1)
 
 
 def lift_y(part, low, x_hi, x_lo, y_recv, table, lhs):
@@ -347,12 +419,11 @@
         for q in range(0, 4, 2):
             columns = []
             for u in (q, q + 1):
-                x = 16 * part + 4 * u + i
-                at = 8 * (x // 2) if low else LOW_ROWS + 8 * (x // 4)
+                x = first + 16 * part + 4 * u + i
+                at = 8 * (x // 4)
                 tiles = jnp.concatenate([y_recv[0, at : at + 8], y_recv[1, at : at + 8]], 0)
-                columns.append(stacked(x_hi[first + x], x_lo[first + x], tiles))
-            which = i % 2 if low else i
-            hi, lo = split(dot(table[which], jnp.concatenate(columns, 1)))
+                columns.append(stacked(x_hi[x], x_lo[x], tiles))
+            hi, lo = split(dot(table[i], jnp.concatenate(columns, 1)))
             for u in (0, 1):
                 lhs[0, part, i, q + u] = hi[:, 128 * u : 128 * u + 128]
                 lhs[1, part, i, q + u] = lo[:, 128 * u : 128 * u + 128]
@@ -365,7 +436,7 @@
     return dot(jnp.concatenate([hi, lo, hi, zh], 1), table[i])
 
 
-def low_part(part, lhs, zh_low, wf, wc, fine, level):
+def low_part(part, lhs, more, zh_low, wf, wc, fine, level):
     for i in range(4):
         one = lift_z(part, i, zh_low, lhs, wf, 0, 64)
         two = lift_z(part, i, zh_low, lhs, wc, 64, 32)
@@ -374,7 +445,7 @@
             fine[0, x] = one[64 * q : 64 * q + 32, 128:192]
             fine[1, x] = one[64 * q + 32 : 64 * q + 64, :64]
             fine[2, x] = one[64 * q + 32 : 64 * q + 64, 128:192]
-            level[x] = two[32 * q : 32 * q + 32]
+            level[x] = two[32 * q : 32 * q + 32] + more[x]
 
 
 def high_part(part, lhs, zh_high, wf, fine):
@@ -397,15 +468,14 @@
                         16 * by : 16 * by + 16, 32 * bz : 32 * bz + 32
                     ]
 
-    lift_loop(HX // 2, 8, lambda i: level[i], store)
+    lift_loop(HX // 2, 16, lambda i: level[i], store)
 
 
 def finish_kernel(
-    lhs_low, lhs_high, z_recv, c_recv, y_low, wf, wc, p_low, p_high,
+    lhs_low, lhs_high, more, z_recv, c_recv, z_one, z_two, z_high, wf, wc, places,
     fine_hbm, coarse_hbm,
     fine, coarse, level, zh_low, zh_high, sem,
 ):
-    lift_z_halos(z_recv, c_recv, y_low, p_low, p_high, zh_low, zh_high)
     copies = []
 
     def write(bands, part):
@@ -414,8 +484,9 @@
         copies.append(pltpu.make_async_copy(src, dst, sem.at[part + (4 if bands == HIGH_BANDS else 0)]))
         copies[-1].start()
 
+    lift_z_halos(z_recv, c_recv, z_one, z_two, z_high, places, zh_low, zh_high)
     for part in range(4):
-        low_part(part, lhs_low, zh_low, wf, wc, fine, level)
+        low_part(part, lhs_low, more, zh_low, wf, wc, fine, level)
         write(LOW_BANDS, part)
     lift_level(level, coarse)
     copies.append(pltpu.make_async_copy(coarse, coarse_hbm, sem.at[8]))
@@ -435,25 +506,26 @@
     vmem = pl.BlockSpec(memory_space=pltpu.VMEM)
     hbm = pl.BlockSpec(memory_space=pltpu.HBM)
     shape = jax.ShapeDtypeStruct
-    y_shape, z_shape, c_shape = (2, LOW_ROWS + HIGH_ROWS, BZ), (2, 3 * BY, 128), (4, 16, 128)
+    y_shape, z_shape, c_shape = (2, Y_ROWS, BZ), (2, Z_ROWS, 128), (4, 16, 128)
     halos = pl.pallas_call(
         exchange_kernel,
         out_shape=(
             shape((2, 4, 4, 4, 96, 128), BF16), shape((2, 4, 4, 4, 64, 128), BF16),
-            shape(z_shape, F32), shape(c_shape, F32),
+            shape((HX, 32, 128), F32), shape(z_shape, F32), shape(c_shape, F32),
         ),
-        in_specs=[hbm] * 7,
-        out_specs=(vmem,) * 4,
+        in_specs=[hbm] * 10,
+        out_specs=(vmem,) * 5,
         scratch_shapes=[
             pltpu.VMEM((NX, BY, BZ), F32),
             pltpu.VMEM((NX, BY, BZ), BF16),
             pltpu.VMEM((NX, BY, BZ), BF16),
             pltpu.VMEM(y_shape, F32),
             pltpu.VMEM(z_shape, F32),
+            pltpu.VMEM((2, BY, 128), F32),
             pltpu.VMEM(c_shape, F32),
             pltpu.VMEM(y_shape, F32),
             *[pltpu.VMEM(a.shape, BF16) for a in send],
-            pltpu.SemaphoreType.DMA((10,)),
+            pltpu.SemaphoreType.DMA((13,)),
             pltpu.SemaphoreType.DMA((8,)),
             pltpu.SemaphoreType.DMA((8,)),
         ],
@@ -466,7 +538,7 @@
     return pl.pallas_call(
         finish_kernel,
         out_shape=(shape(fine_shape, F32), shape(coarse_shape, F32)),
-        in_specs=[vmem] * 9,
+        in_specs=[vmem] * 11,
         out_specs=(hbm, hbm),
         scratch_shapes=[
             pltpu.VMEM(fine_shape, F32),

time: 26.6 us -> 25.2 us (0.947)
  Pallas kernels: 25.7 us -> 24.3 us
    pallas_call x1, Pallas kernels: 19.7 us -> 18 us  [body(): pl.pallas_call(exchange_kernel, out_shape=(shape((2, 4, 4, 4, 96, 128), B...]
where the time goes in v3:
time: 25.2 us; the launch traced here: 25.1 us
  Pallas kernels  24.3 us (96%)
  between operations  0.73 us (3%)
    pallas_call x1, Pallas kernels, body(): pl.pallas_call(exchange_kernel, out_shape=(shape((2, 4, 4, 4, 96, 128), B...  18 us
    pallas_call x1, Pallas kernels, body(): pl.pallas_call(finish_kernel, out_shape=(shape(fine_shape, F32), shape(co...  6.26 us

profile of v3, /device:TPU:1, one launch (start us, length us, event | category | flops | bytes accessed | tf_op | source)
XLA Modules:
  0.0 25.1 jit_solution(14522360877046132751)
XLA Ops:
  0.6 0.0 copy-start.2
  0.6 0.0 copy-start.1
  0.7 0.0 copy-start
  0.7 0.0 copy-start.4
  0.7 0.0 copy-start.5
  0.7 0.0 copy-start.3
  0.7 18.0 %exchange.1 = (bf16[2,4,4,4,96,128]{5,4,3,2,1,0:T(8,128)(2,1)S(1)}, bf16[2,4,4,4,64,128]{5,4,3,2,1,0:T(8,128)(2,1)S(1)}, f32[64,32,128]{2,1,0:T(8,128)S(1)}, f32[2,160,128]{2,1,0:T(8,128)S(1)}, f32[4,16,128]{2,1,0:T(8,128)S(1)}) custom-call(f32[128,64,128]{2,1,0:T(8,128)} %v_hbm.1, bf16[64,768]{1,0:T(8,128)(2,1)} %constant.30.clone.st_low_hbm, ...), custom_call_target="tpu_custom_call" | custom-call | tf_op jit(solution)/shard_map/exchange/pallas_call | solution.py:510
  18.7 0.0 copy-done.2
  18.8 0.0 copy-done.1
  18.8 0.0 copy-done
  18.8 0.0 copy-done.4
  18.8 0.0 copy-done.5
  18.8 0.0 copy-done.3
  18.8 6.3 %finish.1 = (f32[7,64,32,64]{3,2,1,0:T(8,128)}, f32[8,32,16,32]{3,2,1,0:T(8,128)}) custom-call(bf16[2,4,4,4,96,128]{5,4,3,2,1,0:T(8,128)(2,1)S(1)} %get-tuple-element.7.lhs_low, bf16[2,4,4,4,64,128]{5,4,3,2,1,0:T(8,128)(2,1)S(1)} %get-tuple-element.8.lhs_high, f32[64,32,128]{2,1,0:T(8,128)S(1)} %get-tuple-element.9.more, ...), custom_call_target="tpu_custom_call" | custom-call | tf_op jit(solution)/shard_map/finish/pallas_call | solution.py:538
Async XLA Ops:
  0.6 18.1 %copy-start.2 = (bf16[1024,128]{1,0:T(8,128)(2,1)S(1)}, bf16[1024,128]{1,0:T(8,128)(2,1)}, u32[]{:S(2)}) copy-start(bf16[1024,128]{1,0:T(8,128)(2,1)} %constant.44.clone.places) | copy-start | bytes 786436
  0.6 18.1 %copy-start.1 = (bf16[4,512,128]{2,1,0:T(8,128)(2,1)S(1)}, bf16[4,512,128]{2,1,0:T(8,128)(2,1)}, u32[]{:S(2)}) copy-start(bf16[4,512,128]{2,1,0:T(8,128)(2,1)} %constant.43.clone.wc) | copy-start | bytes 1572868
  0.7 18.1 %copy-start = (bf16[4,512,256]{2,1,0:T(8,128)(2,1)S(1)}, bf16[4,512,256]{2,1,0:T(8,128)(2,1)}, u32[]{:S(2)}) copy-start(bf16[4,512,256]{2,1,0:T(8,128)(2,1)} %constant.42.clone.wf) | copy-start | bytes 3145732
  0.7 18.1 %copy-start.4 = (bf16[64,240]{1,0:T(8,128)(2,1)S(1)}, bf16[64,240]{1,0:T(8,128)(2,1)}, u32[]{:S(2)}) copy-start(bf16[64,240]{1,0:T(8,128)(2,1)} %constant.41.clone.z_high) | copy-start | bytes 92164
  0.7 18.1 %copy-start.5 = (bf16[32,96]{1,0:T(8,128)(2,1)S(1)}, bf16[32,96]{1,0:T(8,128)(2,1)}, u32[]{:S(2)}) copy-start(bf16[32,96]{1,0:T(8,128)(2,1)} %constant.40.clone.z_two) | copy-start | bytes 18436
  0.7 18.1 %copy-start.3 = (bf16[96,288]{1,0:T(8,128)(2,1)S(1)}, bf16[96,288]{1,0:T(8,128)(2,1)}, u32[]{:S(2)}) copy-start(bf16[96,288]{1,0:T(8,128)(2,1)} %constant.39.clone.z_one) | copy-start | bytes 165892

commit v4 on v3

--- a/solution.py
+++ b/solution.py
@@ -351,9 +351,9 @@
     for k in (7, 8, 9):
         loads[k].wait()
     find_z_states(x_hi, x_lo, zs_low, zs_high, coarse_y, z_send, z_raw)
-    z_copies = [send(k) for k in (2, 3)]
     find_corners(z_send, z_raw, st_low, c_send)
-    z_copies += [send(k) for k in range(4, 8)]
+    z_copies = [send(k) for k in range(4, 8)]
+    z_copies += [send(k) for k in (2, 3)]
 
     for k in (10, 11, 12):
         loads[k].wait()

time: 25.2 us -> 24.3 us (0.964)
  Pallas kernels: 24.3 us -> 23.2 us
    pallas_call x1, Pallas kernels: 18 us -> 16.9 us  [body(): pl.pallas_call(exchange_kernel, out_shape=(shape((2, 4, 4, 4, 96, 128), B...]
where the time goes in v4:
time: 24.3 us; the launch traced here: 24 us
  Pallas kernels  23.2 us (95%)
  between operations  0.73 us (3%)
    pallas_call x1, Pallas kernels, body(): pl.pallas_call(exchange_kernel, out_shape=(shape((2, 4, 4, 4, 96, 128), B...  16.9 us
    pallas_call x1, Pallas kernels, body(): pl.pallas_call(finish_kernel, out_shape=(shape(fine_shape, F32), shape(co...  6.26 us

profile of v4, /device:TPU:1, one launch (start us, length us, event | category | flops | bytes accessed | tf_op | source)
XLA Modules:
  0.0 24.0 jit_solution(16454950374356867838)
XLA Ops:
  0.6 0.0 copy-start.2
  0.6 0.0 copy-start.1
  0.7 0.0 copy-start
  0.7 0.0 copy-start.4
  0.7 0.0 copy-start.5
  0.7 0.0 copy-start.3
  0.7 16.9 %exchange.1 = (bf16[2,4,4,4,96,128]{5,4,3,2,1,0:T(8,128)(2,1)S(1)}, bf16[2,4,4,4,64,128]{5,4,3,2,1,0:T(8,128)(2,1)S(1)}, f32[64,32,128]{2,1,0:T(8,128)S(1)}, f32[2,160,128]{2,1,0:T(8,128)S(1)}, f32[4,16,128]{2,1,0:T(8,128)S(1)}) custom-call(f32[128,64,128]{2,1,0:T(8,128)} %v_hbm.1, bf16[64,768]{1,0:T(8,128)(2,1)} %constant.30.clone.st_low_hbm, ...), custom_call_target="tpu_custom_call" | custom-call | tf_op jit(solution)/shard_map/exchange/pallas_call | solution.py:510
  17.6 0.0 copy-done.2
  17.7 0.0 copy-done.1
  17.7 0.0 copy-done
  17.7 0.0 copy-done.4
  17.7 0.0 copy-done.5
  17.7 0.0 copy-done.3
  17.7 6.3 %finish.1 = (f32[7,64,32,64]{3,2,1,0:T(8,128)}, f32[8,32,16,32]{3,2,1,0:T(8,128)}) custom-call(bf16[2,4,4,4,96,128]{5,4,3,2,1,0:T(8,128)(2,1)S(1)} %get-tuple-element.7.lhs_low, bf16[2,4,4,4,64,128]{5,4,3,2,1,0:T(8,128)(2,1)S(1)} %get-tuple-element.8.lhs_high, f32[64,32,128]{2,1,0:T(8,128)S(1)} %get-tuple-element.9.more, ...), custom_call_target="tpu_custom_call" | custom-call | tf_op jit(solution)/shard_map/finish/pallas_call | solution.py:538
Async XLA Ops:
  0.6 17.0 %copy-start.2 = (bf16[1024,128]{1,0:T(8,128)(2,1)S(1)}, bf16[1024,128]{1,0:T(8,128)(2,1)}, u32[]{:S(2)}) copy-start(bf16[1024,128]{1,0:T(8,128)(2,1)} %constant.44.clone.places) | copy-start | bytes 786436
  0.6 17.0 %copy-start.1 = (bf16[4,512,128]{2,1,0:T(8,128)(2,1)S(1)}, bf16[4,512,128]{2,1,0:T(8,128)(2,1)}, u32[]{:S(2)}) copy-start(bf16[4,512,128]{2,1,0:T(8,128)(2,1)} %constant.43.clone.wc) | copy-start | bytes 1572868
  0.7 17.0 %copy-start = (bf16[4,512,256]{2,1,0:T(8,128)(2,1)S(1)}, bf16[4,512,256]{2,1,0:T(8,128)(2,1)}, u32[]{:S(2)}) copy-start(bf16[4,512,256]{2,1,0:T(8,128)(2,1)} %constant.42.clone.wf) | copy-start | bytes 3145732
  0.7 17.0 %copy-start.4 = (bf16[64,240]{1,0:T(8,128)(2,1)S(1)}, bf16[64,240]{1,0:T(8,128)(2,1)}, u32[]{:S(2)}) copy-start(bf16[64,240]{1,0:T(8,128)(2,1)} %constant.41.clone.z_high) | copy-start | bytes 92164
  0.7 17.0 %copy-start.5 = (bf16[32,96]{1,0:T(8,128)(2,1)S(1)}, bf16[32,96]{1,0:T(8,128)(2,1)}, u32[]{:S(2)}) copy-start(bf16[32,96]{1,0:T(8,128)(2,1)} %constant.40.clone.z_two) | copy-start | bytes 18436
  0.7 17.0 %copy-start.3 = (bf16[96,288]{1,0:T(8,128)(2,1)S(1)}, bf16[96,288]{1,0:T(8,128)(2,1)}, u32[]{:S(2)}) copy-start(bf16[96,288]{1,0:T(8,128)(2,1)} %constant.39.clone.z_one) | copy-start | bytes 165892

commit v5 on v4

--- a/solution.py
+++ b/solution.py
@@ -485,15 +485,29 @@
         copies[-1].start()
 
     lift_z_halos(z_recv, c_recv, z_one, z_two, z_high, places, zh_low, zh_high)
-    for part in range(4):
+
+    def low(part):
         low_part(part, lhs_low, more, zh_low, wf, wc, fine, level)
         write(LOW_BANDS, part)
-    lift_level(level, coarse)
-    copies.append(pltpu.make_async_copy(coarse, coarse_hbm, sem.at[8]))
-    copies[-1].start()
-    for part in range(4):
+
+    def high(part):
         high_part(part, lhs_high, zh_high, wf, fine)
         write(HIGH_BANDS, part)
+
+    def last():
+        lift_level(level, coarse)
+        copies.append(pltpu.make_async_copy(coarse, coarse_hbm, sem.at[8]))
+        copies[-1].start()
+
+    high(0)
+    high(1)
+    low(0)
+    low(1)
+    low(2)
+    low(3)
+    last()
+    high(2)
+    high(3)
     for copy in copies:
         copy.wait()
 

time: 24.3 us -> 23.8 us (0.979)
  Pallas kernels: 23.2 us -> 22.7 us
    pallas_call x1, Pallas kernels: 6.26 us -> 5.77 us  [body(): pl.pallas_call(finish_kernel, out_shape=(shape(fine_shape, F32), shape(co...]
where the time goes in v5:
time: 23.8 us; the launch traced here: 23.5 us
  Pallas kernels  22.7 us (95%)
  between operations  0.73 us (3%)
    pallas_call x1, Pallas kernels, body(): pl.pallas_call(exchange_kernel, out_shape=(shape((2, 4, 4, 4, 96, 128), B...  16.9 us
    pallas_call x1, Pallas kernels, body(): pl.pallas_call(finish_kernel, out_shape=(shape(fine_shape, F32), shape(co...  5.77 us

profile of v5, /device:TPU:1, one launch (start us, length us, event | category | flops | bytes accessed | tf_op | source)
XLA Modules:
  0.0 23.5 jit_solution(14519604434745764532)
XLA Ops:
  0.6 0.0 copy-start.2
  0.6 0.0 copy-start.1
  0.7 0.0 copy-start
  0.7 0.0 copy-start.4
  0.7 0.0 copy-start.5
  0.7 0.0 copy-start.3
  0.7 16.9 %exchange.1 = (bf16[2,4,4,4,96,128]{5,4,3,2,1,0:T(8,128)(2,1)S(1)}, bf16[2,4,4,4,64,128]{5,4,3,2,1,0:T(8,128)(2,1)S(1)}, f32[64,32,128]{2,1,0:T(8,128)S(1)}, f32[2,160,128]{2,1,0:T(8,128)S(1)}, f32[4,16,128]{2,1,0:T(8,128)S(1)}) custom-call(f32[128,64,128]{2,1,0:T(8,128)} %v_hbm.1, bf16[64,768]{1,0:T(8,128)(2,1)} %constant.30.clone.st_low_hbm, ...), custom_call_target="tpu_custom_call" | custom-call | tf_op jit(solution)/shard_map/exchange/pallas_call | solution.py:524
  17.6 0.0 copy-done.2
  17.7 0.0 copy-done.1
  17.7 0.0 copy-done
  17.7 0.0 copy-done.4
  17.7 0.0 copy-done.5
  17.7 0.0 copy-done.3
  17.7 5.8 %finish.1 = (f32[7,64,32,64]{3,2,1,0:T(8,128)}, f32[8,32,16,32]{3,2,1,0:T(8,128)}) custom-call(bf16[2,4,4,4,96,128]{5,4,3,2,1,0:T(8,128)(2,1)S(1)} %get-tuple-element.7.lhs_low, bf16[2,4,4,4,64,128]{5,4,3,2,1,0:T(8,128)(2,1)S(1)} %get-tuple-element.8.lhs_high, f32[64,32,128]{2,1,0:T(8,128)S(1)} %get-tuple-element.9.more, ...), custom_call_target="tpu_custom_call" | custom-call | tf_op jit(solution)/shard_map/finish/pallas_call | solution.py:552
Async XLA Ops:
  0.6 17.0 %copy-start.2 = (bf16[1024,128]{1,0:T(8,128)(2,1)S(1)}, bf16[1024,128]{1,0:T(8,128)(2,1)}, u32[]{:S(2)}) copy-start(bf16[1024,128]{1,0:T(8,128)(2,1)} %constant.44.clone.places) | copy-start | bytes 786436
  0.6 17.0 %copy-start.1 = (bf16[4,512,128]{2,1,0:T(8,128)(2,1)S(1)}, bf16[4,512,128]{2,1,0:T(8,128)(2,1)}, u32[]{:S(2)}) copy-start(bf16[4,512,128]{2,1,0:T(8,128)(2,1)} %constant.43.clone.wc) | copy-start | bytes 1572868
  0.7 17.0 %copy-start = (bf16[4,512,256]{2,1,0:T(8,128)(2,1)S(1)}, bf16[4,512,256]{2,1,0:T(8,128)(2,1)}, u32[]{:S(2)}) copy-start(bf16[4,512,256]{2,1,0:T(8,128)(2,1)} %constant.42.clone.wf) | copy-start | bytes 3145732
  0.7 17.0 %copy-start.4 = (bf16[64,240]{1,0:T(8,128)(2,1)S(1)}, bf16[64,240]{1,0:T(8,128)(2,1)}, u32[]{:S(2)}) copy-start(bf16[64,240]{1,0:T(8,128)(2,1)} %constant.41.clone.z_high) | copy-start | bytes 92164
  0.7 17.0 %copy-start.5 = (bf16[32,96]{1,0:T(8,128)(2,1)S(1)}, bf16[32,96]{1,0:T(8,128)(2,1)}, u32[]{:S(2)}) copy-start(bf16[32,96]{1,0:T(8,128)(2,1)} %constant.40.clone.z_two) | copy-start | bytes 18436
  0.7 17.0 %copy-start.3 = (bf16[96,288]{1,0:T(8,128)(2,1)S(1)}, bf16[96,288]{1,0:T(8,128)(2,1)}, u32[]{:S(2)}) copy-start(bf16[96,288]{1,0:T(8,128)(2,1)} %constant.39.clone.z_one) | copy-start | bytes 165892

commit v6 on v5

--- a/solution.py
+++ b/solution.py
@@ -468,7 +468,7 @@
                         16 * by : 16 * by + 16, 32 * bz : 32 * bz + 32
                     ]
 
-    lift_loop(HX // 2, 16, lambda i: level[i], store)
+    lift_loop(HX // 2, 32, lambda i: level[i], store)
 
 
 def finish_kernel(

time: 23.8 us -> 23.6 us (level)
  no operation moved by 1% of the time
where the time goes in v6:
time: 23.6 us; the launch traced here: 23.2 us
  Pallas kernels  22.5 us (95%)
  between operations  0.73 us (3%)
    pallas_call x1, Pallas kernels, body(): pl.pallas_call(exchange_kernel, out_shape=(shape((2, 4, 4, 4, 96, 128), B...  16.9 us
    pallas_call x1, Pallas kernels, body(): pl.pallas_call(finish_kernel, out_shape=(shape(fine_shape, F32), shape(co...  5.53 us

profile of v6, /device:TPU:1, one launch (start us, length us, event | category | flops | bytes accessed | tf_op | source)
XLA Modules:
  0.0 23.2 jit_solution(2408287183101401678)
XLA Ops:
  0.6 0.0 copy-start.2
  0.6 0.0 copy-start.1
  0.7 0.0 copy-start
  0.7 0.0 copy-start.4
  0.7 0.0 copy-start.5
  0.7 0.0 copy-start.3
  0.7 16.9 %exchange.1 = (bf16[2,4,4,4,96,128]{5,4,3,2,1,0:T(8,128)(2,1)S(1)}, bf16[2,4,4,4,64,128]{5,4,3,2,1,0:T(8,128)(2,1)S(1)}, f32[64,32,128]{2,1,0:T(8,128)S(1)}, f32[2,160,128]{2,1,0:T(8,128)S(1)}, f32[4,16,128]{2,1,0:T(8,128)S(1)}) custom-call(f32[128,64,128]{2,1,0:T(8,128)} %v_hbm.1, bf16[64,768]{1,0:T(8,128)(2,1)} %constant.30.clone.st_low_hbm, ...), custom_call_target="tpu_custom_call" | custom-call | tf_op jit(solution)/shard_map/exchange/pallas_call | solution.py:524
  17.6 0.0 copy-done.2
  17.7 0.0 copy-done.1
  17.7 0.0 copy-done
  17.7 0.0 copy-done.4
  17.7 0.0 copy-done.5
  17.7 0.0 copy-done.3
  17.7 5.5 %finish.1 = (f32[7,64,32,64]{3,2,1,0:T(8,128)}, f32[8,32,16,32]{3,2,1,0:T(8,128)}) custom-call(bf16[2,4,4,4,96,128]{5,4,3,2,1,0:T(8,128)(2,1)S(1)} %get-tuple-element.7.lhs_low, bf16[2,4,4,4,64,128]{5,4,3,2,1,0:T(8,128)(2,1)S(1)} %get-tuple-element.8.lhs_high, f32[64,32,128]{2,1,0:T(8,128)S(1)} %get-tuple-element.9.more, ...), custom_call_target="tpu_custom_call" | custom-call | tf_op jit(solution)/shard_map/finish/pallas_call | solution.py:552
Async XLA Ops:
  0.6 17.0 %copy-start.2 = (bf16[1024,128]{1,0:T(8,128)(2,1)S(1)}, bf16[1024,128]{1,0:T(8,128)(2,1)}, u32[]{:S(2)}) copy-start(bf16[1024,128]{1,0:T(8,128)(2,1)} %constant.44.clone.places) | copy-start | bytes 786436
  0.6 17.0 %copy-start.1 = (bf16[4,512,128]{2,1,0:T(8,128)(2,1)S(1)}, bf16[4,512,128]{2,1,0:T(8,128)(2,1)}, u32[]{:S(2)}) copy-start(bf16[4,512,128]{2,1,0:T(8,128)(2,1)} %constant.43.clone.wc) | copy-start | bytes 1572868
  0.7 17.0 %copy-start = (bf16[4,512,256]{2,1,0:T(8,128)(2,1)S(1)}, bf16[4,512,256]{2,1,0:T(8,128)(2,1)}, u32[]{:S(2)}) copy-start(bf16[4,512,256]{2,1,0:T(8,128)(2,1)} %constant.42.clone.wf) | copy-start | bytes 3145732
  0.7 17.0 %copy-start.4 = (bf16[64,240]{1,0:T(8,128)(2,1)S(1)}, bf16[64,240]{1,0:T(8,128)(2,1)}, u32[]{:S(2)}) copy-start(bf16[64,240]{1,0:T(8,128)(2,1)} %constant.41.clone.z_high) | copy-start | bytes 92164
  0.7 17.0 %copy-start.5 = (bf16[32,96]{1,0:T(8,128)(2,1)S(1)}, bf16[32,96]{1,0:T(8,128)(2,1)}, u32[]{:S(2)}) copy-start(bf16[32,96]{1,0:T(8,128)(2,1)} %constant.40.clone.z_two) | copy-start | bytes 18436
  0.7 17.0 %copy-start.3 = (bf16[96,288]{1,0:T(8,128)(2,1)S(1)}, bf16[96,288]{1,0:T(8,128)(2,1)}, u32[]{:S(2)}) copy-start(bf16[96,288]{1,0:T(8,128)(2,1)} %constant.39.clone.z_one) | copy-start | bytes 165892
